TPU v7x, 512 devices: a whole 4x8x8 slice. The times are simulated.
512 devices in a mesh: exp: 4 (over x), patch: 128 (over z, y, core).
Axes of the slice: x: 4, y: 8, z: 8, core: 2. Of those that a mesh axis runs over, the one named last changes fastest.
Arguments:
- science_flux: float32 [4, 256, 128, 128], P('exp', 'patch'), may hold values from -6 to 6
- science_var: float32 [4, 256, 128, 128], P('exp', 'patch'), may hold values from 0.5 to 2
- templ_flux: float32 [128, 4, 150, 150], P('patch', 'exp'), may hold values from -6 to 6
- templ_var: float32 [128, 4, 150, 150], P('patch', 'exp'), may hold values from 0.5 to 2
- kernel_coefs: float32 [4, 189, 192], P('exp'), may hold values from -3 to 3
- tile_route: int32 [4, 256, 5], P('exp', 'patch'), may hold values from 0 to 188, as said below
Outputs:
- difference: float32 [4, 256, 2, 128, 128], P('exp', 'patch')
Inputs may be any that keep to these rules, and one draw needn't show every extreme that they name: `tile_route`: column 0 lies in 0..4, column 1 in 0..3, columns 2 and 3 in 0..31, column 4 in 0..188. Among the 2 tiles of one exposure on one patch device at most 1 have the same column 0, and some value of column 0 is taken by exactly 1 of them.
All inputs are finite; a program needn't handle non-finite values.
Results may differ from a plain program's by a relative error of at most 0.0003.
Values sent between devices are 32-bit elements; how exact they have to be, the bound alone decides.
A program may use at most 64 MiB of HBM per device.

v0:
```python
import jax
import jax.numpy as jnp
from jax import lax
from jax.sharding import PartitionSpec as P

TILE = 128
HALF = 11
BASES = 32
TERMS = 6
DETS = 189
DET_SIDE = 32
OFFSETS = 5
CAP = 1
KSIZE = 23
PAD = 150


HIGH = lax.Precision.HIGHEST


def passed_along(block, axis, distance):
    devices = range(lax.axis_size(axis))
    route = [((i - distance) % len(devices), i) for i in devices]
    return lax.ppermute(block, axis, route)


def power_of(ratio, degree):
    deg = degree[:, None]
    return jnp.where(
        deg == 0,
        jnp.ones_like(ratio),
        jnp.where(deg == 1, ratio, jnp.where(deg == 2, ratio * ratio, ratio * ratio * ratio)),
    )


def build_tables():
    basis_ids = jnp.arange(BASES)
    sigma = 1.5 + 1.5 * (basis_ids % 2).astype(jnp.float32)
    deg_rows = basis_ids // 2 % 4
    deg_cols = basis_ids // 8 % 4
    lags = (jnp.arange(KSIZE) - HALF).astype(jnp.float32)
    ratio = lags[None, :] / sigma[:, None]
    envelope = jnp.exp(-0.5 * ratio * ratio)
    prow = power_of(ratio, deg_rows) * envelope
    prow = prow / jnp.sum(jnp.abs(prow), 1, keepdims=True)
    pcol = power_of(ratio, deg_cols) * envelope
    pcol = pcol / jnp.sum(jnp.abs(pcol), 1, keepdims=True)
    big_idx = jnp.arange(PAD)[:, None, None]
    small_idx = jnp.arange(TILE)[None, :, None]
    lag_idx = jnp.arange(KSIZE)[None, None, :]
    onehot = (big_idx - small_idx == lag_idx).astype(jnp.float32)
    row_toep = jnp.einsum("bu,iyu->byi", prow, onehot, precision=HIGH).reshape(BASES * TILE, PAD)
    col_toep = jnp.einsum("bv,jxv->bjx", pcol, onehot, precision=HIGH)
    return (prow, pcol, onehot, row_toep, col_toep)


def poly_terms(xs, ys):
    ones = jnp.ones_like(xs * ys)
    return jnp.stack([ones, xs * ones, ys * ones, xs * xs * ones, xs * ys, ys * ys * ones])


def process(tmpl_flux, tmpl_var, sci_flux, sci_var, coef_row, row_pos, col_pos, tables):
    prow, pcol, onehot, row_toep, col_toep = tables
    first = jnp.dot(row_toep, tmpl_flux, precision=HIGH).reshape(BASES, TILE, PAD)
    conv = jnp.einsum("byj,bjx->byx", first, col_toep, precision=HIGH)
    scale = TILE * DET_SIDE * 0.5
    pixels = jnp.arange(TILE).astype(jnp.float32) + 0.5
    xs = (col_pos * TILE + pixels) / scale - 1.0
    ys = (row_pos * TILE + pixels) / scale - 1.0
    terms = poly_terms(xs[None, :], ys[:, None])
    weights = coef_row.reshape(BASES, TERMS)
    mixed = jnp.einsum("bk,byx->kyx", weights, conv, precision=HIGH)
    diff = sci_flux - jnp.sum(mixed * terms, 0)
    cen_x = (col_pos * TILE + TILE * 0.5) / scale - 1.0
    cen_y = (row_pos * TILE + TILE * 0.5) / scale - 1.0
    centre = poly_terms(cen_x, cen_y)
    centre_w = jnp.dot(weights, centre, precision=HIGH)
    kernel = jnp.einsum("b,bu,bv->uv", centre_w, prow, pcol, precision=HIGH)
    squared = kernel * kernel
    wide = jnp.einsum("uv,jxv->ujx", squared, onehot, precision=HIGH)
    shifted = jnp.stack([tmpl_var[lag : lag + TILE] for lag in range(KSIZE)])
    vconv = jnp.einsum("uyj,ujx->yx", shifted, wide, precision=HIGH)
    return (diff, sci_var + vconv)


def per_device(science_flux, science_var, templ_flux, templ_var, kernel_coefs, tile_route):
    route = tile_route[0]
    local_tiles = route.shape[0]
    slots_all = OFFSETS * CAP
    centre_off = OFFSETS // 2
    tmpl_all_flux, tmpl_all_var = (
        lax.all_gather(templ_flux, "exp", axis=1, tiled=True),
        lax.all_gather(templ_var, "exp", axis=1, tiled=True),
    )
    tmpl_all_flux = tmpl_all_flux[0]
    tmpl_all_var = tmpl_all_var[0]
    tables = build_tables()
    det_hot = (route[:, 4][:, None] == jnp.arange(DETS)[None, :]).astype(jnp.float32)
    coef_rows = jnp.dot(det_hot, kernel_coefs[0], precision=HIGH)
    offset_col = route[:, 0]
    off_hot = (offset_col[:, None] == jnp.arange(OFFSETS)[None, :]).astype(jnp.int32)
    rank = jnp.sum((jnp.cumsum(off_hot, 0) - off_hot) * off_hot, 1)
    slot_of_tile = offset_col * CAP + rank
    slot_hot = slot_of_tile[None, :] == jnp.arange(slots_all)[:, None]
    slot_tile = jnp.sum(slot_hot.astype(jnp.int32) * jnp.arange(local_tiles)[None, :], 1)
    slot_live = jnp.any(slot_hot, 1)
    sci_flux = science_flux[0]
    sci_var = science_var[0]
    rows_pos = route[:, 2].astype(jnp.float32)
    cols_pos = route[:, 3].astype(jnp.float32)
    pack_flux = sci_flux[slot_tile]
    pack_var = sci_var[slot_tile]
    pack_coef = coef_rows[slot_tile]
    pack_meta = jnp.stack(
        [
            route[slot_tile, 1].astype(jnp.float32),
            rows_pos[slot_tile],
            cols_pos[slot_tile],
            slot_live.astype(jnp.float32),
        ],
        1,
    )
    outcomes = []
    for offset_index in range(OFFSETS):
        distance = offset_index - centre_off
        lower = offset_index * CAP
        pieces = (
            pack_flux[lower : lower + CAP],
            pack_var[lower : lower + CAP],
            pack_coef[lower : lower + CAP],
            pack_meta[lower : lower + CAP],
        )
        if distance != 0:
            pieces = passed_along((pieces[0], pieces[1], pieces[2], pieces[3]), "patch", distance)

        def owner_tile(item):
            sflux, svar, coef_row, meta = item
            templ_id = meta[0].astype(jnp.int32)

            def compute(operand):
                diff, var = process(
                    tmpl_all_flux[templ_id],
                    tmpl_all_var[templ_id],
                    sflux,
                    svar,
                    coef_row,
                    meta[1],
                    meta[2],
                    tables,
                )
                return jnp.stack([diff, var])

            def skipped(operand):
                return jnp.zeros((2, TILE, TILE), jnp.float32)

            return lax.cond(meta[3] > 0.5, compute, skipped, 0)

        done = lax.map(owner_tile, pieces)
        diff_part = done[:, 0]
        var_part = done[:, 1]
        if distance != 0:
            diff_part, var_part = passed_along((diff_part, var_part), "patch", -distance)
        outcomes.append(jnp.stack([diff_part, var_part], 1))
    result = jnp.concatenate(outcomes, 0)[slot_of_tile]
    return result[None]


def solution(mesh):
    return jax.shard_map(
        per_device,
        mesh=mesh,
        in_specs=(
            P("exp", "patch", None, None),
            P("exp", "patch", None, None),
            P("patch", "exp", None, None),
            P("patch", "exp", None, None),
            P("exp", None, None),
            P("exp", "patch", None),
        ),
        out_specs=P("exp", "patch", None, None, None),
        check_vma=False,
    )
```

profile of v0, /device:TPU:1, one launch (start us, length us, event | category | flops | bytes accessed | tf_op | source)
XLA Modules:
  0.0 509.1 jit_solution(12068103115980909576)
XLA Ops:
  5.7 14.4 %collective-permute-start = (f32[1,4]{0,1:T(4,128)}, f32[1,4]{0,1:T(4,128)}, u32[]{:S(2)}, u32[]{:S(2)}) collective-permute-start(f32[1,4]{0,1:T(4,128)} %get-tuple-element.775), channel_id=1, source_target_pairs={{2,0},{3,1},{4,2},{5,3},{6,4},{7,5},{8,6},{9,7},{10,8},{11,9},{12,... | collective-permute-start | bytes 56 | tf_op jit(solution)/shard_map/ppermute | solution.py:24
  24.0 3.0 collective-permute-start.1
  28.4 3.0 collective-permute-start.2
  32.6 3.0 collective-permute-start.3
  35.6 3.7 collective-permute-start.6
  44.5 3.5 copy.203
  48.0 11.7 %all_gather.7 = f32[1,4,150,150]{3,0,2,1:T(1,128)S(1)} all-gather(f32[1,1,150,150]{3,0,2,1:T(1,128)S(1)} %bitcast.376), channel_id=1, replica_groups=mesh['exp'=4,'patch'=128] {'exp'}, dimensions={1}, use_global_device_ids=true | all-gather | bytes 450000 | tf_op jit(solution)/shard_map/all_gather | solution.py:93
  59.8 10.2 %all_gather.6 = f32[1,4,150,150]{3,0,2,1:T(1,128)S(1)} all-gather(f32[1,1,150,150]{3,0,2,1:T(1,128)S(1)} %bitcast.377), channel_id=1, replica_groups=mesh['exp'=4,'patch'=128] {'exp'}, dimensions={1}, use_global_device_ids=true | all-gather | bytes 450000 | tf_op jit(solution)/shard_map/all_gather | solution.py:92
  72.1 9.0 %conditional.7 = (f32[1,2,128,128]{3,2,1,0:T(8,128)S(1)}) conditional(s32[]{:T(128)} %bitcast.123, () %tuple.51, (f32[5,128,128]{2,1,0:T(8,128)}, f32[5,1]{0,1:T(1,128)}, f32[4,150,150]{2,1,0:T(8,128)}, f32[4096,150]{0,1:T(8,128)}, f32[32,150,128]{2,0,1:T(8,128)S(1)}, /*index=5*/f32[5,192]{1,0:T(8,128)}, f32[5,4]{0,1:T(4,128)S(1)}, ...), branch_computations={%region_12.13_spmd, %region_13.15_spmd} | conditional | flops 2888036864 | bytes 54862964 | solution.py:156
  81.8 7.7 %collective-permute-start.7 = (f32[1,192]{1,0:T(1,128)}, f32[1,192]{1,0:T(1,128)}, u32[]{:S(2)}, u32[]{:S(2)}) collective-permute-start(f32[1,192]{1,0:T(1,128)} %get-tuple-element.770), channel_id=1, source_target_pairs={{1,0},{2,1},{3,2},{4,3},{5,4},{6,5},{7,6},{8,7},{9,8},{10,9},{11,1... | collective-permute-start | bytes 2312 | tf_op jit(solution)/shard_map/ppermute | solution.py:24
  91.3 65.6 %collective-permute-start.12 = (f32[1,4]{0,1:T(4,128)}, f32[1,4]{0,1:T(4,128)S(1)}, u32[]{:S(2)}, u32[]{:S(2)}) collective-permute-start(f32[1,4]{0,1:T(4,128)} %get-tuple-element.773), channel_id=1, source_target_pairs={{127,0},{0,1},{1,2},{2,3},{3,4},{4,5},{5,6},{6,7},{7,8},{8,9},{9,1... | collective-permute-start | bytes 56 | tf_op jit(solution)/shard_map/ppermute | solution.py:24
  161.8 4.8 collective-permute-done.18
  166.6 3.1 collective-permute-start.8
  172.9 3.6 collective-permute-start.13
  178.5 75.6 %conditional.5 = (f32[2,128,128]{2,1,0:T(8,128)S(1)}) conditional(s32[]{:T(128)} %bitcast.104, () %tuple.47, (f32[1,4]{0,1:T(4,128)}, f32[4,150,150]{2,1,0:T(8,128)}, f32[4096,150]{0,1:T(8,128)}, f32[32,150,128]{2,0,1:T(8,128)S(1)}, f32[1,192]{1,0:T(1,128)}, /*index=5*/f32[1,128,128]{2,1,0:T(8,128)}, f32[1,128,128]{2,1,0:T(8,128)}, ...), branch_computations={%region_6.7_spmd, %region_7.9_spmd} | conditional | flops 2888036864 | bytes 54600836 | solution.py:156
  222.8 3.2 fusion.221
  226.1 4.2 fusion.22
  230.3 3.3 fusion.26
  234.3 10.8 %fusion = f32[32,128,128]{2,1,0:T(8,128)} fusion(f32[32,150,128]{2,0,1:T(8,128)S(1)} %get-tuple-element.659, f32[32,128,150]{1,0,2:T(8,128)S(1)} %slice_bitcast_fusion), kind=kOutput, calls=%fused_computation.7 | convolution fusion | flops 943718400 | bytes 7012352 | tf_op jit(solution)/shard_map/while/body/eval_jaxpr/cond/branch_1_fun/byj,bjx->byx/dot_general | solution.py:65
  249.2 4.0 fusion.13
  258.7 2.9 collective-permute-start.20
  261.6 9.0 %conditional.6 = (f32[2,128,128]{2,1,0:T(8,128)S(1)}) conditional(s32[]{:T(128)} %bitcast.117, () %tuple.49, (f32[1,4]{0,1:T(4,128)}, f32[4,150,150]{2,1,0:T(8,128)}, f32[4096,150]{0,1:T(8,128)}, f32[32,150,128]{2,0,1:T(8,128)S(1)}, f32[1,192]{1,0:T(1,128)}, /*index=5*/f32[1,128,128]{2,1,0:T(8,128)}, f32[1,128,128]{2,1,0:T(8,128)}, ...), branch_computations={%region_9.10_spmd, %region_10.12_spmd} | conditional | flops 2888036864 | bytes 54600836 | solution.py:156
  271.3 70.4 %collective-permute-start.21 = (f32[1,128,128]{2,1,0:T(8,128)}, f32[1,128,128]{2,1,0:T(8,128)}, u32[]{:S(2)}, u32[]{:S(2)}) collective-permute-start(f32[1,128,128]{2,1,0:T(8,128)} %get-tuple-element.752), channel_id=1, source_target_pairs={{126,0},{127,1},{0,2},{1,3},{2,4},{3,5},{4,6},{5,7},{6,8},{7,9},{8... | collective-permute-start | bytes 196616 | tf_op jit(solution)/shard_map/ppermute | solution.py:24
  345.6 75.4 %conditional.8 = (f32[2,128,128]{2,1,0:T(8,128)S(1)}) conditional(s32[]{:T(128)} %bitcast.124, () %tuple.53, (f32[1,4]{0,1:T(4,128)}, f32[4,150,150]{2,1,0:T(8,128)}, f32[4096,150]{0,1:T(8,128)}, f32[32,150,128]{2,0,1:T(8,128)S(1)}, f32[1,192]{1,0:T(1,128)}, /*index=5*/f32[1,128,128]{2,1,0:T(8,128)}, f32[1,128,128]{2,1,0:T(8,128)}, ...), branch_computations={%region_15.16_spmd, %region_16.18_spmd} | conditional | flops 2888036864 | bytes 54600836 | solution.py:156
  389.8 3.2 fusion.223
  393.1 4.2 fusion.130
  397.4 3.3 fusion.134
  401.3 10.6 %fusion.108 = f32[32,128,128]{2,1,0:T(8,128)} fusion(f32[32,150,128]{2,0,1:T(8,128)S(1)} %get-tuple-element.693, f32[32,128,150]{1,0,2:T(8,128)S(1)} %slice_bitcast_fusion.3), kind=kOutput, calls=%fused_computation.176 | convolution fusion | flops 943718400 | bytes 7012352 | tf_op jit(solution)/shard_map/while/body/eval_jaxpr/cond/branch_1_fun/byj,bjx->byx/dot_general | solution.py:65
  416.0 4.0 fusion.121
  421.7 3.0 collective-permute-start.10
  430.5 67.6 %collective-permute-start.17 = (f32[1,128,128]{2,1,0:T(8,128)}, f32[1,128,128]{2,1,0:T(8,128)S(1)}, u32[]{:S(2)}, u32[]{:S(2)}) collective-permute-start(f32[1,128,128]{2,1,0:T(8,128)} %get-tuple-element.763), channel_id=1, source_target_pairs={{1,0},{2,1},{3,2},{4,3},{5,4},{6,5},{7,6},{8,7},{9,8},{10,9},{11,1... | collective-permute-start | bytes 196616 | tf_op jit(solution)/shard_map/ppermute | solution.py:24
  498.1 3.3 collective-permute-start.22
  (220 shorter events, 147.0 us)
Async XLA Ops:
  0.0 27.0 %copy-start = (f32[1,2,128,128]{3,2,1,0:T(8,128)S(1)}, f32[1,2,128,128]{3,2,1,0:T(8,128)}, u32[]{:S(2)}) copy-start(f32[1,2,128,128]{3,2,1,0:T(8,128)} %param.16) | copy-start | bytes 393220
  0.0 31.3 %copy-start.14 = (f32[1,2,128,128]{3,2,1,0:T(8,128)S(1)}, f32[1,2,128,128]{3,2,1,0:T(8,128)}, u32[]{:S(2)}) copy-start(f32[1,2,128,128]{3,2,1,0:T(8,128)} %param.17) | copy-start | bytes 393220
  5.0 15.1 %copy-start.30 = (f32[5,1]{0,1:T(1,128)}, f32[5,1]{0,1:T(1,128)S(1)}, u32[]{:S(2)}) copy-start(f32[5,1]{0,1:T(1,128)S(1)} %convert_bitcast_fusion) | copy-start | bytes 64
  5.7 76.2 %collective-permute-start = (f32[1,4]{0,1:T(4,128)}, f32[1,4]{0,1:T(4,128)}, u32[]{:S(2)}, u32[]{:S(2)}) collective-permute-start(f32[1,4]{0,1:T(4,128)} %get-tuple-element.775), channel_id=1, source_target_pairs={{2,0},{3,1},{4,2},{5,3},{6,4},{7,5},{8,6},{9,7},{10,8},{11,9},{12,... | collective-permute-start | bytes 56 | tf_op jit(solution)/shard_map/ppermute | solution.py:24
  24.0 147.0 %collective-permute-start.1 = (f32[1,192]{1,0:T(1,128)}, f32[1,192]{1,0:T(1,128)}, u32[]{:S(2)}, u32[]{:S(2)}) collective-permute-start(f32[1,192]{1,0:T(1,128)} %get-tuple-element.771), channel_id=1, source_target_pairs={{2,0},{3,1},{4,2},{5,3},{6,4},{7,5},{8,6},{9,7},{10,8},{11,9},{12,... | collective-permute-start | bytes 2312 | tf_op jit(solution)/shard_map/ppermute | solution.py:24
  27.6 12.6 %copy-start.13 = (f32[5,128,128]{2,1,0:T(8,128)}, f32[5,128,128]{2,1,0:T(8,128)S(1)}, u32[]{:S(2)}) copy-start(f32[5,128,128]{2,1,0:T(8,128)S(1)} %gather_fusion.4) | copy-start | bytes 983044
  28.4 144.6 %collective-permute-start.2 = (f32[1,128,128]{2,1,0:T(8,128)}, f32[1,128,128]{2,1,0:T(8,128)}, u32[]{:S(2)}, u32[]{:S(2)}) collective-permute-start(f32[1,128,128]{2,1,0:T(8,128)} %get-tuple-element.759), channel_id=1, source_target_pairs={{2,0},{3,1},{4,2},{5,3},{6,4},{7,5},{8,6},{9,7},{10,8},{11,9},{12,... | collective-permute-start | bytes 196616 | tf_op jit(solution)/shard_map/ppermute | solution.py:24
  32.6 143.9 %collective-permute-start.3 = (f32[1,128,128]{2,1,0:T(8,128)}, f32[1,128,128]{2,1,0:T(8,128)}, u32[]{:S(2)}, u32[]{:S(2)}) collective-permute-start(f32[1,128,128]{2,1,0:T(8,128)} %get-tuple-element.755), channel_id=1, source_target_pairs={{2,0},{3,1},{4,2},{5,3},{6,4},{7,5},{8,6},{9,7},{10,8},{11,9},{12,... | collective-permute-start | bytes 196616 | tf_op jit(solution)/shard_map/ppermute | solution.py:24
  35.6 55.7 %collective-permute-start.6 = (f32[1,4]{0,1:T(4,128)}, f32[1,4]{0,1:T(4,128)}, u32[]{:S(2)}, u32[]{:S(2)}) collective-permute-start(f32[1,4]{0,1:T(4,128)} %get-tuple-element.774), channel_id=1, source_target_pairs={{1,0},{2,1},{3,2},{4,3},{5,4},{6,5},{7,6},{8,7},{9,8},{10,9},{11,1... | collective-permute-start | bytes 56 | tf_op jit(solution)/shard_map/ppermute | solution.py:24
  81.8 173.0 %collective-permute-start.7 = (f32[1,192]{1,0:T(1,128)}, f32[1,192]{1,0:T(1,128)}, u32[]{:S(2)}, u32[]{:S(2)}) collective-permute-start(f32[1,192]{1,0:T(1,128)} %get-tuple-element.770), channel_id=1, source_target_pairs={{1,0},{2,1},{3,2},{4,3},{5,4},{6,5},{7,6},{8,7},{9,8},{10,9},{11,1... | collective-permute-start | bytes 2312 | tf_op jit(solution)/shard_map/ppermute | solution.py:24
  91.3 67.4 %collective-permute-start.12 = (f32[1,4]{0,1:T(4,128)}, f32[1,4]{0,1:T(4,128)S(1)}, u32[]{:S(2)}, u32[]{:S(2)}) collective-permute-start(f32[1,4]{0,1:T(4,128)} %get-tuple-element.773), channel_id=1, source_target_pairs={{127,0},{0,1},{1,2},{2,3},{3,4},{4,5},{5,6},{6,7},{7,8},{8,9},{9,1... | collective-permute-start | bytes 56 | tf_op jit(solution)/shard_map/ppermute | solution.py:24
  158.7 19.8 %copy-start.29 = (f32[1,4]{0,1:T(4,128)}, f32[1,4]{0,1:T(4,128)S(1)}, u32[]{:S(2)}) copy-start(f32[1,4]{0,1:T(4,128)S(1)} %collective-permute-done.12) | copy-start | bytes 52
  158.7 7.9 %collective-permute-start.18 = (f32[1,4]{0,1:T(4,128)}, f32[1,4]{0,1:T(4,128)S(1)}, u32[]{:S(2)}, u32[]{:S(2)}) collective-permute-start(f32[1,4]{0,1:T(4,128)} %get-tuple-element.772), channel_id=1, source_target_pairs={{126,0},{127,1},{0,2},{1,3},{2,4},{3,5},{4,6},{5,7},{6,8},{7,9},{8... | collective-permute-start | bytes 56 | tf_op jit(solution)/shard_map/ppermute | solution.py:24
  166.6 90.2 %collective-permute-start.8 = (f32[1,128,128]{2,1,0:T(8,128)}, f32[1,128,128]{2,1,0:T(8,128)}, u32[]{:S(2)}, u32[]{:S(2)}) collective-permute-start(f32[1,128,128]{2,1,0:T(8,128)} %get-tuple-element.758), channel_id=1, source_target_pairs={{1,0},{2,1},{3,2},{4,3},{5,4},{6,5},{7,6},{8,7},{9,8},{10,9},{11,1... | collective-permute-start | bytes 196616 | tf_op jit(solution)/shard_map/ppermute | solution.py:24
  171.0 87.7 %collective-permute-start.9 = (f32[1,128,128]{2,1,0:T(8,128)}, f32[1,128,128]{2,1,0:T(8,128)}, u32[]{:S(2)}, u32[]{:S(2)}) collective-permute-start(f32[1,128,128]{2,1,0:T(8,128)} %get-tuple-element.754), channel_id=1, source_target_pairs={{1,0},{2,1},{3,2},{4,3},{5,4},{6,5},{7,6},{8,7},{9,8},{10,9},{11,1... | collective-permute-start | bytes 196616 | tf_op jit(solution)/shard_map/ppermute | solution.py:24
  172.9 98.4 %collective-permute-start.13 = (f32[1,192]{1,0:T(1,128)}, f32[1,192]{1,0:T(1,128)}, u32[]{:S(2)}, u32[]{:S(2)}) collective-permute-start(f32[1,192]{1,0:T(1,128)} %get-tuple-element.769), channel_id=1, source_target_pairs={{127,0},{0,1},{1,2},{2,3},{3,4},{4,5},{5,6},{6,7},{7,8},{8,9},{9,1... | collective-permute-start | bytes 2312 | tf_op jit(solution)/shard_map/ppermute | solution.py:24
  176.6 165.1 %collective-permute-start.14 = (f32[1,128,128]{2,1,0:T(8,128)}, f32[1,128,128]{2,1,0:T(8,128)}, u32[]{:S(2)}, u32[]{:S(2)}) collective-permute-start(f32[1,128,128]{2,1,0:T(8,128)} %get-tuple-element.757), channel_id=1, source_target_pairs={{127,0},{0,1},{1,2},{2,3},{3,4},{4,5},{5,6},{6,7},{7,8},{8,9},{9,1... | collective-permute-start | bytes 196616 | tf_op jit(solution)/shard_map/ppermute | solution.py:24
  183.2 39.4 %copy-start.16 = (f32[32,23]{0,1:T(8,128)S(1)}, f32[32,23]{0,1:T(8,128)}, u32[]{:S(2)}) copy-start(f32[32,23]{0,1:T(8,128)} %get-tuple-element.384) | copy-start | bytes 8836 | tf_op jit(solution)/shard_map/while/body/eval_jaxpr/cond
  254.9 88.8 %collective-permute-start.15 = (f32[1,128,128]{2,1,0:T(8,128)}, f32[1,128,128]{2,1,0:T(8,128)}, u32[]{:S(2)}, u32[]{:S(2)}) collective-permute-start(f32[1,128,128]{2,1,0:T(8,128)} %get-tuple-element.753), channel_id=1, source_target_pairs={{127,0},{0,1},{1,2},{2,3},{3,4},{4,5},{5,6},{6,7},{7,8},{8,9},{9,1... | collective-permute-start | bytes 196616 | tf_op jit(solution)/shard_map/ppermute | solution.py:24
  256.8 164.9 %collective-permute-start.19 = (f32[1,192]{1,0:T(1,128)}, f32[1,192]{1,0:T(1,128)}, u32[]{:S(2)}, u32[]{:S(2)}) collective-permute-start(f32[1,192]{1,0:T(1,128)} %get-tuple-element.768), channel_id=1, source_target_pairs={{126,0},{127,1},{0,2},{1,3},{2,4},{3,5},{4,6},{5,7},{6,8},{7,9},{8... | collective-permute-start | bytes 2312 | tf_op jit(solution)/shard_map/ppermute | solution.py:24
  258.7 166.0 %collective-permute-start.20 = (f32[1,128,128]{2,1,0:T(8,128)}, f32[1,128,128]{2,1,0:T(8,128)}, u32[]{:S(2)}, u32[]{:S(2)}) collective-permute-start(f32[1,128,128]{2,1,0:T(8,128)} %get-tuple-element.756), channel_id=1, source_target_pairs={{126,0},{127,1},{0,2},{1,3},{2,4},{3,5},{4,6},{5,7},{6,8},{7,9},{8... | collective-permute-start | bytes 196616 | tf_op jit(solution)/shard_map/ppermute | solution.py:24
  271.3 155.3 %collective-permute-start.21 = (f32[1,128,128]{2,1,0:T(8,128)}, f32[1,128,128]{2,1,0:T(8,128)}, u32[]{:S(2)}, u32[]{:S(2)}) collective-permute-start(f32[1,128,128]{2,1,0:T(8,128)} %get-tuple-element.752), channel_id=1, source_target_pairs={{126,0},{127,1},{0,2},{1,3},{2,4},{3,5},{4,6},{5,7},{6,8},{7,9},{8... | collective-permute-start | bytes 196616 | tf_op jit(solution)/shard_map/ppermute | solution.py:24
  341.7 88.7 %collective-permute-start.4 = (f32[1,128,128]{2,1,0:T(8,128)}, f32[1,128,128]{2,1,0:T(8,128)}, u32[]{:S(2)}, u32[]{:S(2)}) collective-permute-start(f32[1,128,128]{2,1,0:T(8,128)} %get-tuple-element.766), channel_id=1, source_target_pairs={{126,0},{127,1},{0,2},{1,3},{2,4},{3,5},{4,6},{5,7},{6,8},{7,9},{8... | collective-permute-start | bytes 196616 | tf_op jit(solution)/shard_map/ppermute | solution.py:24
  343.7 154.4 %collective-permute-start.5 = (f32[1,128,128]{2,1,0:T(8,128)}, f32[1,128,128]{2,1,0:T(8,128)}, u32[]{:S(2)}, u32[]{:S(2)}) collective-permute-start(f32[1,128,128]{2,1,0:T(8,128)} %get-tuple-element.767), channel_id=1, source_target_pairs={{126,0},{127,1},{0,2},{1,3},{2,4},{3,5},{4,6},{5,7},{6,8},{7,9},{8... | collective-permute-start | bytes 196616 | tf_op jit(solution)/shard_map/ppermute | solution.py:24
  350.4 39.3 %copy-start.18 = (f32[32,23]{0,1:T(8,128)S(1)}, f32[32,23]{0,1:T(8,128)}, u32[]{:S(2)}) copy-start(f32[32,23]{0,1:T(8,128)} %get-tuple-element.418) | copy-start | bytes 8836 | tf_op jit(solution)/shard_map/while/body/eval_jaxpr/cond
  421.7 80.5 %collective-permute-start.10 = (f32[1,128,128]{2,1,0:T(8,128)}, f32[1,128,128]{2,1,0:T(8,128)}, u32[]{:S(2)}, u32[]{:S(2)}) collective-permute-start(f32[1,128,128]{2,1,0:T(8,128)} %get-tuple-element.764), channel_id=1, source_target_pairs={{127,0},{0,1},{1,2},{2,3},{3,4},{4,5},{5,6},{6,7},{7,8},{8,9},{9,1... | collective-permute-start | bytes 196616 | tf_op jit(solution)/shard_map/ppermute | solution.py:24
  424.7 80.2 %collective-permute-start.11 = (f32[1,128,128]{2,1,0:T(8,128)}, f32[1,128,128]{2,1,0:T(8,128)}, u32[]{:S(2)}, u32[]{:S(2)}) collective-permute-start(f32[1,128,128]{2,1,0:T(8,128)} %get-tuple-element.765), channel_id=1, source_target_pairs={{127,0},{0,1},{1,2},{2,3},{3,4},{4,5},{5,6},{6,7},{7,8},{8,9},{9,1... | collective-permute-start | bytes 196616 | tf_op jit(solution)/shard_map/ppermute | solution.py:24
  426.7 79.2 %collective-permute-start.16 = (f32[1,128,128]{2,1,0:T(8,128)}, f32[1,128,128]{2,1,0:T(8,128)}, u32[]{:S(2)}, u32[]{:S(2)}) collective-permute-start(f32[1,128,128]{2,1,0:T(8,128)} %get-tuple-element.762), channel_id=1, source_target_pairs={{1,0},{2,1},{3,2},{4,3},{5,4},{6,5},{7,6},{8,7},{9,8},{10,9},{11,1... | collective-permute-start | bytes 196616 | tf_op jit(solution)/shard_map/ppermute | solution.py:24
  430.4 78.1 %copy-start.1 = (f32[1,2,128,128]{3,2,1,0:T(8,128)S(1)}, f32[1,2,128,128]{3,2,1,0:T(8,128)}, u32[]{:S(2)}) copy-start(f32[1,2,128,128]{3,2,1,0:T(8,128)} %param.16) | copy-start | bytes 393220
  430.5 75.4 %collective-permute-start.17 = (f32[1,128,128]{2,1,0:T(8,128)}, f32[1,128,128]{2,1,0:T(8,128)S(1)}, u32[]{:S(2)}, u32[]{:S(2)}) collective-permute-start(f32[1,128,128]{2,1,0:T(8,128)} %get-tuple-element.763), channel_id=1, source_target_pairs={{1,0},{2,1},{3,2},{4,3},{5,4},{6,5},{7,6},{8,7},{9,8},{10,9},{11,1... | collective-permute-start | bytes 196616 | tf_op jit(solution)/shard_map/ppermute | solution.py:24
  498.1 8.7 %collective-permute-start.22 = (f32[1,128,128]{2,1,0:T(8,128)S(1)}, f32[1,128,128]{2,1,0:T(8,128)S(1)}, u32[]{:S(2)}, u32[]{:S(2)}) collective-permute-start(f32[1,128,128]{2,1,0:T(8,128)S(1)} %get-tuple-element.760), channel_id=1, source_target_pairs={{2,0},{3,1},{4,2},{5,3},{6,4},{7,5},{8,6},{9,7},{10,8},{11,9},{12,... | collective-permute-start | bytes 196616 | tf_op jit(solution)/shard_map/ppermute | solution.py:24
  502.3 5.0 collective-permute-start.23
  (10 other events, 53.0 us)
where the time goes:
time: 519 us; the launch traced here: 509 us
  starting transfers between devices  275 us (53%)
  local copies, waits for them, and re-layouts  110 us (21%)
  matrix products  55.2 us (11%)
  loops' own time  23.9 us (5%)
  blocking collectives  21.9 us (4%)
  other arithmetic  13.4 us (3%)
  waiting for transfers between devices  5.31 us (1%)
    ppermute x24, starting transfers between devices, passed_along(): return lax.ppermute(block, axis, route)  275 us
    cond x62, local copies, waits for them, and re-layouts  72.4 us
    another operation x5, loops' own time, owner_tile(): return lax.cond(meta[3] > 0.5, compute, skipped, 0)  23.9 us
    dot_general x2, matrix products, process(): conv = jnp.einsum('byj,bjx->byx', first, col_toep, precision=HIGH)  21.5 us
    all_gather x1, blocking collectives, per_device(): lax.all_gather(templ_var, 'exp', axis=1, tiled=True)  11.7 us
  transfers between devices with their start and end apart: 24, of which 2 were waited for; matrix products, arithmetic and copies ran while one was open for 34% of the time, Pallas kernels for 0%

commit v1 on v0

v1 whole, which is shorter than its diff:
```python
import functools

import jax
import jax.numpy as jnp
import ml_dtypes
import numpy as np
from jax import lax
from jax.experimental import pallas as pl
from jax.experimental.pallas import tpu as pltpu
from jax.sharding import PartitionSpec as P

TILE = 128
HALF = 11
KSIZE = 23
PAD = 150
BASES = 32
TERMS = 6
DET_SIDE = 32
COLS = BASES * TERMS
MAIN = 152
REM = PAD - TILE
PACKED = MAIN + 32
GROUPS = 5
ROWS = 160
HALF_A = 96
CENTRE = 2
SCALE = TILE * DET_SIDE * 0.5
MESH = pl.DeviceIdType.MESH
BF16 = jnp.bfloat16
F32 = jnp.float32
HIGH = lax.Precision.HIGHEST


def split_np(x):
    hi = x.astype(np.float32).astype(ml_dtypes.bfloat16)
    lo = (x - hi.astype(np.float64)).astype(ml_dtypes.bfloat16)
    return hi, lo


def make_tables():
    lags = np.arange(KSIZE) - HALF
    prof = np.zeros((8, KSIZE))
    for s in range(2):
        for m in range(4):
            ratio = lags / (1.5 + 1.5 * s)
            row = ratio**m * np.exp(-0.5 * ratio * ratio)
            prof[s * 4 + m] = row / np.abs(row).sum()
    toep = np.zeros((8, PAD, TILE))
    for u in range(KSIZE):
        for x in range(TILE):
            toep[:, x + u, x] = prof[:, u]
    cols = toep.transpose(1, 0, 2).reshape(PAD, 8 * TILE)
    hi, lo = split_np(cols)
    ca = np.zeros((4 * TILE, 8 * TILE), ml_dtypes.bfloat16)
    ca[0:128] = hi[:128]
    ca[128:256] = hi[:128]
    ca[256:384] = lo[:128]
    ca[384 : 384 + REM] = hi[128:]
    ca[416 : 416 + REM] = hi[128:]
    ca[448 : 448 + REM] = lo[128:]
    rows = np.zeros((TILE, 8, ROWS))
    rows[:, :, :PAD] = toep.transpose(2, 0, 1)
    hi, lo = split_np(rows.reshape(TILE, 8 * ROWS))
    rh = np.concatenate([hi, lo], 0)
    xdeg = [0, 1, 0, 2, 1, 0]
    ydeg = [0, 0, 1, 0, 1, 2]
    pick = np.zeros((96, COLS), np.float32)
    pick2 = np.zeros((8, COLS), np.float32)
    deg = np.zeros((COLS, TILE), np.float32)
    rev = np.zeros((COLS, TILE), np.float32)
    term = np.zeros((8, COLS), np.float32)
    for b in range(BASES):
        s, mx, my = b % 2, b // 2 % 4, b // 8 % 4
        for k in range(TERMS):
            col = b * TERMS + k
            pick[((s * 4 + mx) * 3 + ydeg[k]) * 4 + my, col] = 1
            pick2[s * 4 + mx, col] = 1
            deg[col] = xdeg[k]
            term[:, col] = k
            for v in range(KSIZE):
                rev[col, -v % TILE] = prof[s * 4 + my, v]
    prow = np.zeros((24, 8), np.float32)
    prow[:KSIZE] = prof.T
    return ca, rh, pick, pick2, deg, rev, term, prow


def exchange_kernel(route, tf, tv, sel, raw, gath, ysend, recv, rqs, rqr, ld_sem, xs, xr, ys, yr, rs, rr):
    e = lax.axis_index("exp")
    p = lax.axis_index("patch")
    ne = lax.axis_size("exp")
    npatch = lax.axis_size("patch")
    right = (lax.rem(e + 1, ne), p)
    left = (lax.rem(e + ne - 1, ne), p)

    def along(d):
        return (e, lax.rem(p + d + npatch, npatch))

    loads = [pltpu.make_async_copy(src, raw.at[c], ld_sem.at[c]) for c, src in enumerate((tf, tv))]
    for load in loads:
        load.start()
    barrier = pltpu.get_barrier_semaphore()
    others = [right, left] + [along(d) for d in (-2, -1, 1, 2)]
    for other in others:
        pl.semaphore_signal(barrier, inc=1, device_id=other, device_id_type=MESH)

    ids = []
    for k in range(5):
        want = jnp.int32(0)
        for t in range(2):
            want = jnp.where(route[t, 0] == k, route[t, 1], want)
        want = lax.rem(want - e + ne, ne)
        ids.append(want)
        rqs[k] = jnp.full((8, TILE), want, jnp.int32)

    lane = lax.broadcasted_iota(jnp.int32, (32, TILE), 1)
    for c in range(2):
        loads[c].wait()
        gath[c, 0, 0:PAD, :] = raw[c, :, 0:TILE]
        gath[c, 0, PAD:MAIN, :] = jnp.zeros((MAIN - PAD, TILE), F32)
        packed = jnp.zeros((32, TILE), F32)
        for g in range(GROUPS):
            n = min(32, PAD - 32 * g)
            part = raw[c, 32 * g : 32 * g + n, TILE:PAD]
            part = jnp.concatenate([part, jnp.zeros((n, TILE - REM), F32)], 1)
            if n < 32:
                part = jnp.concatenate([part, jnp.zeros((32 - n, TILE), F32)], 0)
            if g:
                part = pltpu.roll(part, REM * g, 1)
            packed = packed + part
        gath[c, 0, MAIN:PACKED, :] = packed

    pl.semaphore_wait(barrier, len(others))

    def copy(src, dst, ssem, rsem, to):
        return pltpu.make_async_remote_copy(
            src_ref=src, dst_ref=dst, send_sem=ssem, recv_sem=rsem, device_id=to, device_id_type=MESH
        )

    part_a = pl.ds(0, HALF_A)
    part_b = pl.ds(HALF_A, PACKED - HALF_A)
    sends = []
    asks = {}
    for d in (-2, -1, 1, 2):
        k = d + CENTRE
        asks[k] = copy(rqs.at[k], rqr.at[k], rs.at[k], rr.at[k], along(d))
        asks[k].start()
    firsts = []
    for c in range(2):
        mine = gath.at[c, 0]
        four = [
            copy(mine.at[part_a], gath.at[c, 3, part_a], xs.at[c, 0], xr.at[c, 0], right),
            copy(mine.at[part_b], gath.at[c, 1, part_b], xs.at[c, 1], xr.at[c, 1], left),
            copy(mine.at[part_b], gath.at[c, 3, part_b], xs.at[c, 2], xr.at[c, 2], right),
            copy(mine.at[part_a], gath.at[c, 1, part_a], xs.at[c, 3], xr.at[c, 3], left),
        ]
        for one in four:
            one.start()
        firsts.append(four)
    for d in (-2, -1, 1, 2):
        asks[d + CENTRE].wait()
    answers = []
    for c in range(2):
        four = firsts[c]
        relays = []
        four[0].wait_recv()
        relays.append(copy(gath.at[c, 3, part_a], gath.at[c, 2, part_a], xs.at[c, 4], xr.at[c, 4], right))
        relays[0].start()
        four[1].wait_recv()
        relays.append(copy(gath.at[c, 1, part_b], gath.at[c, 2, part_b], xs.at[c, 5], xr.at[c, 5], left))
        relays[1].start()
        four[2].wait_recv()
        four[3].wait_recv()
        relays[0].wait_recv()
        relays[1].wait_recv()
        sends += four + relays
        for k in (0, 4, 1, 3, 2):
            asked = rqr[k, 0:1, :] if k != CENTRE else rqs[k, 0:1, :]
            asked = jnp.broadcast_to(asked, (PACKED, TILE))
            value = gath[c, 3]
            for j in (2, 1, 0):
                value = jnp.where(asked == j, gath[c, j], value)
            if k == CENTRE:
                recv[c, k] = value
            else:
                ysend[c, k] = value
                answer = copy(ysend.at[c, k], recv.at[c, k], ys.at[c, k], yr.at[c, k], along(CENTRE - k))
                answer.start()
                answers.append(answer)
    for one in answers:
        one.wait_recv()
    for t in range(2):
        for c in range(2):
            sel[t, c] = recv[c, route[t, 0]]
    for one in sends + answers:
        one.wait_send()


def fill_lhs(src, dst):
    main = src[0:MAIN, :]
    main = jnp.concatenate([main, jnp.zeros((ROWS - MAIN, TILE), F32)], 0)
    hi = main.astype(BF16)
    dst[:, 0:128] = hi
    dst[:, 128:256] = (main - hi.astype(F32)).astype(BF16)
    dst[:, 256:384] = hi
    other = src[MAIN:PACKED, :]
    lane = lax.broadcasted_iota(jnp.int32, (32, TILE), 1)
    for g in range(GROUPS):
        part = pltpu.roll(other, TILE - REM * g, 1) if g else other
        part = jnp.where(lane < REM, part, 0.0)
        hi = part.astype(BF16).astype(F32)
        part = hi + pltpu.roll(part - hi, 32, 1) + pltpu.roll(hi, 64, 1)
        dst[32 * g : 32 * g + 32, 384:512] = part.astype(BF16)


def prepare(t, route, kc, pick, pick2, deg, rev, term, prow, alpha, toep):
    coefs = kc[pl.ds(route[t, 4], 1), :]
    row = route[t, 2].astype(F32)
    col = route[t, 3].astype(F32)
    lanes = lax.broadcasted_iota(jnp.int32, (1, TILE), 1).astype(F32)
    xs = (col * TILE + lanes + 0.5) / SCALE - 1.0
    powers = jnp.where(deg[...] == 0.0, 1.0, jnp.where(deg[...] == 1.0, xs, xs * xs))
    alpha[t] = jnp.dot(pick[...] * coefs, powers, precision=HIGH, preferred_element_type=F32)
    cx = (col * TILE + TILE * 0.5) / SCALE - 1.0
    cy = (row * TILE + TILE * 0.5) / SCALE - 1.0
    kinds = term[...]
    centre = jnp.where(kinds == 0.0, 1.0, 0.0)
    for k, value in enumerate((cx, cy, cx * cx, cx * cy, cy * cy)):
        centre = jnp.where(kinds == k + 1.0, value, centre)
    mixed = jnp.dot(pick2[...] * centre * coefs, rev[...], precision=HIGH, preferred_element_type=F32)
    kernel = jnp.dot(prow[...], mixed, precision=HIGH, preferred_element_type=F32)
    squared = kernel * kernel
    sub = lax.broadcasted_iota(jnp.int32, (32, TILE), 0)
    lane = lax.broadcasted_iota(jnp.int32, (32, TILE), 1)
    low = lane <= sub
    for u in range(KSIZE):
        at = ((u % 8) * 3 + u // 8) * TILE
        at = slice(at, at + TILE)
        base = jnp.broadcast_to(squared[u : u + 1, :], (TILE, TILE))
        circ = pltpu.roll(base, 0, 1, stride=1, stride_axis=0)
        top = circ[0:32]
        main = jnp.concatenate([jnp.where(low, top, 0.0), circ[32:]], 0)
        rest = jnp.where(low, 0.0, top)
        hi = main.astype(BF16)
        toep[t, 0:128, at] = hi
        toep[t, 128:256, at] = hi
        toep[t, 256:384, at] = (main - hi.astype(F32)).astype(BF16)
        hi = rest.astype(BF16)
        toep[t, 384:416, at] = hi
        toep[t, 416:448, at] = hi
        toep[t, 448:480, at] = (rest - hi.astype(F32)).astype(BF16)
        toep[t, 480:512, at] = jnp.zeros((32, TILE), BF16)


def mix_columns(t, lhs, ca, hbuf, alpha, uh, ul):
    hbuf[...] = jnp.dot(lhs[...], ca[...], preferred_element_type=F32)

    def chunk(i, carry):
        at = pl.ds(pl.multiple_of(i * 16, 16), 16)
        for s in range(2):
            parts = [hbuf[at, (s * 4 + my) * TILE : (s * 4 + my + 1) * TILE] for my in range(4)]
            for mx in range(4):
                for j in range(3):
                    first = ((s * 4 + mx) * 3 + j) * 4
                    total = alpha[t, first : first + 1, :] * parts[0]
                    for my in range(1, 4):
                        total = total + alpha[t, first + my : first + my + 1, :] * parts[my]
                    to = pl.ds(pl.multiple_of((s * 4 + mx) * ROWS + i * 16, 16), 16)
                    cols = slice((t * 3 + j) * TILE, (t * 3 + j + 1) * TILE)
                    hi = total.astype(BF16)
                    uh[to, cols] = hi
                    ul[to, cols] = (total - hi.astype(F32)).astype(BF16)
        return carry

    lax.fori_loop(0, ROWS // 16, chunk, 0)


def rows_of(t, route, z):
    row = route[t, 2].astype(F32)
    subs = lax.broadcasted_iota(jnp.int32, (TILE, TILE), 0).astype(F32)
    ys = (row * TILE + subs + 0.5) / SCALE - 1.0
    z = z[:, t * 384 : (t + 1) * 384]
    return z[:, 0:128] + ys * (z[:, 128:256] + ys * z[:, 256:384])


def variance(t, lhs, toep):
    acc = jnp.zeros((TILE, TILE), F32)
    for r in range(8):
        width = 384 if r < 7 else 256
        part = jnp.dot(lhs[...], toep[t, :, r * 384 : r * 384 + width], preferred_element_type=F32)
        total = part[0:136, 0:128] + part[8:144, 128:256]
        if width == 384:
            total = total + part[16:152, 256:384]
        acc = acc + total[r : r + TILE]
    return acc


def compute_kernel(route, sel, sf, sv, kc, ca, rh, pick, pick2, deg, rev, term, prow, out, lhs, alpha, toep, hbuf, uh, ul):
    for t in range(2):
        prepare(t, route, kc, pick, pick2, deg, rev, term, prow, alpha, toep)
    for t in range(2):
        fill_lhs(sel.at[t, 0], lhs)
        mix_columns(t, lhs, ca, hbuf, alpha, uh, ul)
    z = jnp.dot(rh[...], uh[...], preferred_element_type=F32)
    z = z[0:128] + z[128:256] + jnp.dot(rh[0:128, :], ul[...], preferred_element_type=F32)
    for t in range(2):
        out[t, 0] = sf[t] - rows_of(t, route, z)
    for t in range(2):
        fill_lhs(sel.at[t, 1], lhs)
        out[t, 1] = sv[t] + variance(t, lhs, toep)


def per_device(science_flux, science_var, templ_flux, templ_var, kernel_coefs, tile_route):
    route = tile_route[0]
    vmem = pl.BlockSpec(memory_space=pltpu.VMEM)
    smem = pl.BlockSpec(memory_space=pltpu.SMEM)
    hbm = pl.BlockSpec(memory_space=pl.ANY)
    dma = pltpu.SemaphoreType.DMA
    sel = pl.pallas_call(
        exchange_kernel,
        out_shape=jax.ShapeDtypeStruct((2, 2, PACKED, TILE), F32),
        in_specs=[smem, hbm, hbm],
        out_specs=vmem,
        scratch_shapes=[
            pltpu.VMEM((2, PAD, PAD), F32),
            pltpu.VMEM((2, 4, PACKED, TILE), F32),
            pltpu.VMEM((2, 5, PACKED, TILE), F32),
            pltpu.VMEM((2, 5, PACKED, TILE), F32),
            pltpu.VMEM((5, 8, TILE), jnp.int32),
            pltpu.VMEM((5, 8, TILE), jnp.int32),
            dma((2,)),
            dma((2, 6)),
            dma((2, 6)),
            dma((2, 5)),
            dma((2, 5)),
            dma((5,)),
            dma((5,)),
        ],
        compiler_params=pltpu.CompilerParams(
            collective_id=0, has_side_effects=True, vmem_limit_bytes=32 * 2**20
        ),
        name="exchange",
    )(route, templ_flux[0, 0], templ_var[0, 0])
    tables = [jnp.asarray(x) for x in make_tables()]
    out = pl.pallas_call(
        compute_kernel,
        out_shape=jax.ShapeDtypeStruct((2, 2, TILE, TILE), F32),
        in_specs=[smem] + [vmem] * (4 + len(tables)),
        out_specs=vmem,
        scratch_shapes=[
            pltpu.VMEM((ROWS, 512), BF16),
            pltpu.VMEM((2, 96, TILE), F32),
            pltpu.VMEM((2, 512, 24 * TILE), BF16),
            pltpu.VMEM((ROWS, 1024), F32),
            pltpu.VMEM((8 * ROWS, 768), BF16),
            pltpu.VMEM((8 * ROWS, 768), BF16),
        ],
        compiler_params=pltpu.CompilerParams(vmem_limit_bytes=48 * 2**20),
        name="convolve",
    )(route, sel, science_flux[0], science_var[0], kernel_coefs[0], *tables)
    return out[None]


def solution(mesh):
    return jax.shard_map(
        per_device,
        mesh=mesh,
        in_specs=(
            P("exp", "patch", None, None),
            P("exp", "patch", None, None),
            P("patch", "exp", None, None),
            P("patch", "exp", None, None),
            P("exp", None, None),
            P("exp", "patch", None),
        ),
        out_specs=P("exp", "patch", None, None, None),
        check_vma=False,
    )
```

time: 519 us -> 48.7 us (0.09); the launches traced: 509 us -> 48 us
  starting transfers between devices: 275 us -> 0 us
  local copies, waits for them, and re-layouts: 110 us -> 9.32 us
  matrix products: 55.2 us -> 0 us
  Pallas kernels: 0 us -> 38.6 us
  loops' own time: 23.9 us -> 0 us
  blocking collectives: 21.9 us -> 0 us
  other arithmetic: 13.4 us -> 0 us
  waiting for transfers between devices: 5.31 us -> 0 us
    ppermute x24 -> x0, starting transfers between devices: 275 us -> none  [passed_along(): return lax.ppermute(block, axis, route)]
    cond x62 -> x0, local copies, waits for them, and re-layouts: 72.4 us -> none
    dot_general x17 -> x0, matrix products: 55.2 us -> none  [the longest x2 21.5 us: process(): conv = jnp.einsum('byj,bjx->byx', first, col_toep, precision=HIGH)]
    pallas_call x0 -> x2, Pallas kernels: none -> 38.6 us  [the longest x1 30.9 us: per_device(): pl.pallas_call(exchange_kernel, out_shape=jax.ShapeDtypeStruct((2, 2, PAC...]
    another operation x5 -> x0, loops' own time: 23.9 us -> none  [owner_tile(): return lax.cond(meta[3] > 0.5, compute, skipped, 0)]
    all_gather x2 -> x0, blocking collectives: 21.9 us -> none  [the longest x1 11.7 us: per_device(): lax.all_gather(templ_var, 'exp', axis=1, tiled=True)]
    another operation x24 -> x0, local copies, waits for them, and re-layouts: 15.9 us -> none  [the longest x12 6.4 us: poly_terms(): jnp.stack([ones, xs * ones, ys * ones, xs * xs * ones, xs * ys, ys * ys *...]
    slice x12 -> x0, local copies, waits for them, and re-layouts: 8.95 us -> none  [the longest x5 4.04 us: owner_tile(): return lax.cond(meta[3] > 0.5, compute, skipped, 0)]
  transfers between devices with their start and end apart: 24 -> 0, of which waited for: 2 -> 0; matrix products, arithmetic and copies ran while one was open for 34% -> 0% of each run, Pallas kernels for 0% -> 0%
where the time goes in v1:
time: 48.7 us; the launch traced here: 48 us
  Pallas kernels  38.6 us (79%)
  local copies, waits for them, and re-layouts  9.32 us (19%)
    pallas_call x1, Pallas kernels, per_device(): pl.pallas_call(exchange_kernel, out_shape=jax.ShapeDtypeStruct((2, 2, PAC...  30.9 us
    unnamed x26, local copies, waits for them, and re-layouts  9.32 us
    pallas_call x1, Pallas kernels, per_device(): pl.pallas_call(compute_kernel, out_shape=jax.ShapeDtypeStruct((2, 2, TILE...  7.73 us

profile of v1, /device:TPU:1, one launch (start us, length us, event | category | flops | bytes accessed | tf_op | source)
XLA Modules:
  0.0 48.0 jit_solution(8202657317042509939)
XLA Ops:
  0.0 0.0 copy-start
  0.0 1.1 %copy_bitcast_fusion.1 = (f32[150,150]{1,0:T(8,128)S(1)}, f32[150,150]{1,0:T(8,128)S(1)}) fusion(f32[1,1,150,150]{3,1,2,0:T(1,128)} %param.17, f32[1,1,150,150]{3,1,2,0:T(1,128)} %param.16), kind=kLoop, calls=%fused_computation.1 | loop fusion | bytes 360000
  1.1 0.0 copy-start.1
  1.1 0.0 copy-start.10
  1.1 0.7 %copy-done.10 = s32[1,2,5]{2,1,0:T(2,128)S(1)} copy-done((s32[1,2,5]{2,1,0:T(2,128)S(1)}, s32[1,2,5]{2,1,0:T(2,128)}, u32[]{:S(2)}) %copy-start.10) | copy-done | bytes 64
  1.9 30.9 %exchange.1.sel = f32[2,2,184,128]{3,2,1,0:T(8,128)S(1)} custom-call(s32[2,5]{1,0:T(2,128)S(1)} %bitcast.14, f32[150,150]{1,0:T(8,128)S(1)} %get-tuple-element.6.tf, f32[150,150]{1,0:T(8,128)S(1)} %get-tuple-element.5.tv), custom_call_target="tpu_custom_call" | custom-call | tf_op jit(solution)/shard_map/exchange/pallas_call | solution.py:318
  32.8 0.0 copy-start.7
  32.8 0.9 %copy.21 = f32[1,189,192]{2,1,0:T(8,128)S(1)} copy(f32[1,189,192]{2,0,1:T(1,128)} %param.18) | data formatting | bytes 290304
  33.8 0.0 copy-start.11
  33.8 0.0 copy-done
  33.8 0.0 copy-done.1
  33.8 0.0 copy-done.7
  33.8 0.6 %copy-done.11 = s32[1,2,5]{2,1,0:T(2,128)S(1)} copy-done((s32[1,2,5]{2,1,0:T(2,128)S(1)}, s32[1,2,5]{2,1,0:T(2,128)}, u32[]{:S(2)}) %copy-start.11) | copy-done | bytes 64
  34.4 0.0 copy-start.2
  34.4 0.9 %copy-done.2 = f32[1,2,128,128]{3,2,1,0:T(8,128)S(1)} copy-done((f32[1,2,128,128]{3,2,1,0:T(8,128)S(1)}, f32[1,2,128,128]{3,2,1,0:T(8,128)}, u32[]{:S(2)}) %copy-start.2) | copy-done | bytes 131096
  35.3 0.0 copy-start.3
  35.3 0.9 %copy-done.3 = f32[1,2,128,128]{3,2,1,0:T(8,128)S(1)} copy-done((f32[1,2,128,128]{3,2,1,0:T(8,128)S(1)}, f32[1,2,128,128]{3,2,1,0:T(8,128)}, u32[]{:S(2)}) %copy-start.3) | copy-done | bytes 131096
  36.2 0.0 copy-start.4
  36.2 0.9 %copy-done.4 = f32[96,192]{1,0:T(8,128)S(1)} copy-done((f32[96,192]{1,0:T(8,128)S(1)}, f32[96,192]{1,0:T(8,128)}, u32[]{:S(2)}) %copy-start.4) | copy-done | bytes 73752
  37.1 0.0 copy-start.5
  37.1 0.9 %copy-done.5 = f32[192,128]{1,0:T(8,128)S(1)} copy-done((f32[192,128]{1,0:T(8,128)S(1)}, f32[192,128]{1,0:T(8,128)}, u32[]{:S(2)}) %copy-start.5) | copy-done | bytes 98328
  38.0 0.0 copy-start.6
  38.0 0.9 %copy-done.6 = f32[192,128]{1,0:T(8,128)S(1)} copy-done((f32[192,128]{1,0:T(8,128)S(1)}, f32[192,128]{1,0:T(8,128)}, u32[]{:S(2)}) %copy-start.6) | copy-done | bytes 98328
  38.9 0.0 copy-start.8
  38.9 0.7 %copy-done.8 = f32[8,192]{1,0:T(8,128)S(1)} copy-done((f32[8,192]{1,0:T(8,128)S(1)}, f32[8,192]{1,0:T(8,128)}, u32[]{:S(2)}) %copy-start.8) | copy-done | bytes 6168
  39.6 0.0 copy-start.9
  39.6 0.7 %copy-done.9 = f32[8,192]{1,0:T(8,128)S(1)} copy-done((f32[8,192]{1,0:T(8,128)S(1)}, f32[8,192]{1,0:T(8,128)}, u32[]{:S(2)}) %copy-start.9) | copy-done | bytes 6168
  40.3 7.7 %convolve.1 = f32[2,2,128,128]{3,2,1,0:T(8,128)} custom-call(s32[2,5]{1,0:T(2,128)S(1)} %bitcast.15, f32[2,2,184,128]{3,2,1,0:T(8,128)S(1)} %exchange.1.sel, f32[2,128,128]{2,1,0:T(8,128)S(1)} %bitcast.12, f32[2,128,128]{2,1,0:T(8,128)S(1)} %bitcast.13, f32[189,192]{1,0:T(8,128)S(1)} %bitcast.11, bf16[512,1024]{1,0:T(8,128)(2,1)S(1)} %copy-done, ...), custom_call_target="tpu_custom_call" | custom-call | tf_op jit(solution)/shard_map/convolve/pallas_call | solution.py:344
Async XLA Ops:
  0.0 33.8 %copy-start = (bf16[512,1024]{1,0:T(8,128)(2,1)S(1)}, bf16[512,1024]{1,0:T(8,128)(2,1)}, u32[]{:S(2)}) copy-start(bf16[512,1024]{1,0:T(8,128)(2,1)} %constant.16.clone.ca) | copy-start | bytes 3145732
  1.1 32.7 %copy-start.1 = (bf16[256,1280]{1,0:T(8,128)(2,1)S(1)}, bf16[256,1280]{1,0:T(8,128)(2,1)}, u32[]{:S(2)}) copy-start(bf16[256,1280]{1,0:T(8,128)(2,1)} %constant.17.clone.rh) | copy-start | bytes 1966084
  1.1 0.7 %copy-start.10 = (s32[1,2,5]{2,1,0:T(2,128)S(1)}, s32[1,2,5]{2,1,0:T(2,128)}, u32[]{:S(2)}) copy-start(s32[1,2,5]{2,1,0:T(2,128)} %param.19) | copy-start | bytes 124
  32.8 1.0 %copy-start.7 = (f32[24,8]{1,0:T(8,128)S(1)}, f32[24,8]{1,0:T(8,128)}, u32[]{:S(2)}) copy-start(f32[24,8]{1,0:T(8,128)} %constant.23.clone.prow) | copy-start | bytes 2308
  33.8 0.7 %copy-start.11 = (s32[1,2,5]{2,1,0:T(2,128)S(1)}, s32[1,2,5]{2,1,0:T(2,128)}, u32[]{:S(2)}) copy-start(s32[1,2,5]{2,1,0:T(2,128)} %param.19) | copy-start | bytes 124
  34.4 0.9 %copy-start.2 = (f32[1,2,128,128]{3,2,1,0:T(8,128)S(1)}, f32[1,2,128,128]{3,2,1,0:T(8,128)}, u32[]{:S(2)}) copy-start(f32[1,2,128,128]{3,2,1,0:T(8,128)} %param.14) | copy-start | bytes 393220
  35.3 0.9 %copy-start.3 = (f32[1,2,128,128]{3,2,1,0:T(8,128)S(1)}, f32[1,2,128,128]{3,2,1,0:T(8,128)}, u32[]{:S(2)}) copy-start(f32[1,2,128,128]{3,2,1,0:T(8,128)} %param.15) | copy-start | bytes 393220
  36.2 0.9 %copy-start.4 = (f32[96,192]{1,0:T(8,128)S(1)}, f32[96,192]{1,0:T(8,128)}, u32[]{:S(2)}) copy-start(f32[96,192]{1,0:T(8,128)} %constant.18.clone.pick) | copy-start | bytes 221188
  37.1 0.9 %copy-start.5 = (f32[192,128]{1,0:T(8,128)S(1)}, f32[192,128]{1,0:T(8,128)}, u32[]{:S(2)}) copy-start(f32[192,128]{1,0:T(8,128)} %constant.20.clone.deg) | copy-start | bytes 294916
  38.0 0.9 %copy-start.6 = (f32[192,128]{1,0:T(8,128)S(1)}, f32[192,128]{1,0:T(8,128)}, u32[]{:S(2)}) copy-start(f32[192,128]{1,0:T(8,128)} %constant.21.clone.rev) | copy-start | bytes 294916
  38.9 0.7 %copy-start.8 = (f32[8,192]{1,0:T(8,128)S(1)}, f32[8,192]{1,0:T(8,128)}, u32[]{:S(2)}) copy-start(f32[8,192]{1,0:T(8,128)} %constant.19.clone.pick2) | copy-start | bytes 18436
  39.6 0.7 %copy-start.9 = (f32[8,192]{1,0:T(8,128)S(1)}, f32[8,192]{1,0:T(8,128)}, u32[]{:S(2)}) copy-start(f32[8,192]{1,0:T(8,128)} %constant.22.clone.term) | copy-start | bytes 18436

commit v2 on v1

v2 whole, which is shorter than its diff:
```python
import jax
import jax.numpy as jnp
import ml_dtypes
import numpy as np
from jax import lax
from jax.experimental import pallas as pl
from jax.experimental.pallas import tpu as pltpu
from jax.sharding import PartitionSpec as P

TILE = 128
HALF = 11
KSIZE = 23
PAD = 150
BASES = 32
TERMS = 6
DET_SIDE = 32
COLS = BASES * TERMS
MAIN = 152
REM = PAD - TILE
PACKED = MAIN + 32
GROUPS = 5
ROWS = 160
CUTS = ((0, 96), (96, PACKED))
N_TABLES = 8
CENTRE = 2
SCALE = TILE * DET_SIDE * 0.5
MESH = pl.DeviceIdType.MESH
BF16 = jnp.bfloat16
F32 = jnp.float32
HIGH = lax.Precision.HIGHEST


def split_np(x):
    hi = x.astype(np.float32).astype(ml_dtypes.bfloat16)
    lo = (x - hi.astype(np.float64)).astype(ml_dtypes.bfloat16)
    return hi, lo


def make_tables():
    lags = np.arange(KSIZE) - HALF
    prof = np.zeros((8, KSIZE))
    for s in range(2):
        for m in range(4):
            ratio = lags / (1.5 + 1.5 * s)
            row = ratio**m * np.exp(-0.5 * ratio * ratio)
            prof[s * 4 + m] = row / np.abs(row).sum()
    toep = np.zeros((8, PAD, TILE))
    for u in range(KSIZE):
        for x in range(TILE):
            toep[:, x + u, x] = prof[:, u]
    cols = toep.transpose(1, 0, 2).reshape(PAD, 8 * TILE)
    hi, lo = split_np(cols)
    ca = np.zeros((4 * TILE, 8 * TILE), ml_dtypes.bfloat16)
    ca[0:128] = hi[:128]
    ca[128:256] = hi[:128]
    ca[256:384] = lo[:128]
    ca[384 : 384 + REM] = hi[128:]
    ca[416 : 416 + REM] = hi[128:]
    ca[448 : 448 + REM] = lo[128:]
    rows = np.zeros((TILE, 8, ROWS))
    rows[:, :, :PAD] = toep.transpose(2, 0, 1)
    hi, lo = split_np(rows.reshape(TILE, 8 * ROWS))
    rh = np.concatenate([hi, lo], 0)
    xdeg = [0, 1, 0, 2, 1, 0]
    ydeg = [0, 0, 1, 0, 1, 2]
    pick = np.zeros((96, COLS), np.float32)
    pick2 = np.zeros((8, COLS), np.float32)
    deg = np.zeros((COLS, TILE), np.float32)
    rev = np.zeros((COLS, TILE), np.float32)
    term = np.zeros((8, COLS), np.float32)
    for b in range(BASES):
        s, mx, my = b % 2, b // 2 % 4, b // 8 % 4
        for k in range(TERMS):
            col = b * TERMS + k
            pick[((s * 4 + mx) * 3 + ydeg[k]) * 4 + my, col] = 1
            pick2[s * 4 + mx, col] = 1
            deg[col] = xdeg[k]
            term[:, col] = k
            for v in range(KSIZE):
                rev[col, -v % TILE] = prof[s * 4 + my, v]
    prow = np.zeros((24, 8), np.float32)
    prow[:KSIZE] = prof.T
    return ca, rh, pick, pick2, deg, rev, term, prow


def fill_lhs(src, dst):
    main = src[0:MAIN]
    main = jnp.concatenate([main, jnp.zeros((ROWS - MAIN, TILE), F32)], 0)
    hi = main.astype(BF16)
    dst[:, 0:128] = hi
    dst[:, 128:256] = (main - hi.astype(F32)).astype(BF16)
    dst[:, 256:384] = hi
    other = src[MAIN:PACKED]
    lane = lax.broadcasted_iota(jnp.int32, (32, TILE), 1)
    for g in range(GROUPS):
        part = pltpu.roll(other, TILE - REM * g, 1) if g else other
        part = jnp.where(lane < REM, part, 0.0)
        hi = part.astype(BF16).astype(F32)
        part = hi + pltpu.roll(part - hi, 32, 1) + pltpu.roll(hi, 64, 1)
        dst[32 * g : 32 * g + 32, 384:512] = part.astype(BF16)


def prepare(t, route, kc, pick, pick2, deg, rev, term, prow, alpha, square, toep):
    coefs = kc[route[t, 4]]
    row = route[t, 2].astype(F32)
    col = route[t, 3].astype(F32)
    lanes = lax.broadcasted_iota(jnp.int32, (1, TILE), 1).astype(F32)
    xs = (col * TILE + lanes + 0.5) / SCALE - 1.0
    powers = jnp.where(deg[...] == 0.0, 1.0, jnp.where(deg[...] == 1.0, xs, xs * xs))
    alpha[t] = jnp.dot(pick[...] * coefs, powers, precision=HIGH, preferred_element_type=F32)
    cx = (col * TILE + TILE * 0.5) / SCALE - 1.0
    cy = (row * TILE + TILE * 0.5) / SCALE - 1.0
    kinds = term[...]
    centre = jnp.where(kinds == 0.0, 1.0, 0.0)
    for k, value in enumerate((cx, cy, cx * cx, cx * cy, cy * cy)):
        centre = jnp.where(kinds == k + 1.0, value, centre)
    mixed = jnp.dot(pick2[...] * centre * coefs, rev[...], precision=HIGH, preferred_element_type=F32)
    kernel = jnp.dot(prow[...], mixed, precision=HIGH, preferred_element_type=F32)
    sub = lax.broadcasted_iota(jnp.int32, (32, TILE), 0)
    lane = lax.broadcasted_iota(jnp.int32, (32, TILE), 1)
    low = lane <= sub
    square[t] = kernel * kernel

    def lag(u, carry):
        at = pl.ds(pl.multiple_of((lax.rem(u, 8) * 3 + lax.div(u, 8)) * TILE, TILE), TILE)
        base = jnp.broadcast_to(square[t, pl.ds(u, 1), :], (TILE, TILE))
        circ = pltpu.roll(base, 0, 1, stride=1, stride_axis=0)
        top = circ[0:32]
        main = jnp.concatenate([jnp.where(low, top, 0.0), circ[32:]], 0)
        rest = jnp.where(low, 0.0, top)
        hi = main.astype(BF16)
        toep[t, 0:128, at] = hi
        toep[t, 128:256, at] = hi
        toep[t, 256:384, at] = (main - hi.astype(F32)).astype(BF16)
        hi = rest.astype(BF16)
        toep[t, 384:416, at] = hi
        toep[t, 416:448, at] = hi
        toep[t, 448:480, at] = (rest - hi.astype(F32)).astype(BF16)
        toep[t, 480:512, at] = jnp.zeros((32, TILE), BF16)
        return carry

    lax.fori_loop(0, KSIZE, lag, 0)


def mix_columns(t, lhs, ca, hbuf, alpha, uh, ul):
    hbuf[...] = jnp.dot(lhs[...], ca[...], preferred_element_type=F32)

    def chunk(i, carry):
        at = pl.ds(pl.multiple_of(i * 16, 16), 16)
        for s in range(2):
            parts = [hbuf[at, (s * 4 + my) * TILE : (s * 4 + my + 1) * TILE] for my in range(4)]
            for mx in range(4):
                for j in range(3):
                    first = ((s * 4 + mx) * 3 + j) * 4
                    total = alpha[t, first : first + 1, :] * parts[0]
                    for my in range(1, 4):
                        total = total + alpha[t, first + my : first + my + 1, :] * parts[my]
                    to = pl.ds(pl.multiple_of((s * 4 + mx) * ROWS + i * 16, 16), 16)
                    cols = slice((t * 3 + j) * TILE, (t * 3 + j + 1) * TILE)
                    hi = total.astype(BF16)
                    uh[to, cols] = hi
                    ul[to, cols] = (total - hi.astype(F32)).astype(BF16)
        return carry

    lax.fori_loop(0, ROWS // 16, chunk, 0)


def rows_of(t, route, z):
    row = route[t, 2].astype(F32)
    subs = lax.broadcasted_iota(jnp.int32, (TILE, TILE), 0).astype(F32)
    ys = (row * TILE + subs + 0.5) / SCALE - 1.0
    z = z[:, t * 384 : (t + 1) * 384]
    return z[:, 0:128] + ys * (z[:, 128:256] + ys * z[:, 256:384])


def variance(t, lhs, toep):
    acc = jnp.zeros((TILE, TILE), F32)
    for r in range(8):
        width = 384 if r < 7 else 256
        part = jnp.dot(lhs[...], toep[t, :, r * 384 : r * 384 + width], preferred_element_type=F32)
        total = part[0:136, 0:128] + part[8:144, 128:256]
        if width == 384:
            total = total + part[16:152, 256:384]
        acc = acc + total[r : r + TILE]
    return acc


def fetch(refs, buffers, sem):
    copies = [pltpu.make_async_copy(src, dst, sem.at[i]) for i, (src, dst) in enumerate(zip(refs, buffers))]
    for one in copies:
        one.start()
    return copies


def pack(raw, dst):
    dst[0:PAD, :] = raw[:, 0:TILE]
    dst[PAD:MAIN, :] = jnp.zeros((MAIN - PAD, TILE), F32)
    packed = jnp.zeros((32, TILE), F32)
    for g in range(GROUPS):
        n = min(32, PAD - 32 * g)
        part = raw[32 * g : 32 * g + n, TILE:PAD]
        part = jnp.concatenate([part, jnp.zeros((n, TILE - REM), F32)], 1)
        if n < 32:
            part = jnp.concatenate([part, jnp.zeros((32 - n, TILE), F32)], 0)
        if g:
            part = pltpu.roll(part, REM * g, 1)
        packed = packed + part
    dst[MAIN:PACKED, :] = packed


def difference_kernel(*refs):
    n = N_TABLES
    tf, tv, route_in, kc_in = refs[:4]
    tables_in, out = refs[4 : 4 + n], refs[4 + n]
    raw, route, kc = refs[5 + n : 8 + n]
    tables = refs[8 + n : 8 + 2 * n]
    gath, ysend, recv_flux, recv_var, rqs, rqr, lhs, alpha, square, toep, hbuf, uh, ul = refs[8 + 2 * n : 21 + 2 * n]
    ld_sem, tab_sem, xs, xr, ys, yr, rs, rr = refs[21 + 2 * n :]
    recv = (recv_flux, recv_var)
    ca, rh, pick, pick2, deg, rev, term, prow = tables

    e = lax.axis_index("exp")
    p = lax.axis_index("patch")
    ne = lax.axis_size("exp")
    npatch = lax.axis_size("patch")
    exposures = {k: (lax.rem(e + k, ne), p) for k in (2, 1, 3)}

    def along(d):
        return (e, lax.rem(p + d + npatch, npatch))

    barrier = pltpu.get_barrier_semaphore()
    others = list(exposures.values()) + [along(d) for d in (-2, -1, 1, 2)]
    for other in others:
        pl.semaphore_signal(barrier, inc=1, device_id=other, device_id_type=MESH)
    loads = fetch((tf.at[:, 0, :], tv.at[:, 0, :], route_in, kc_in), (raw.at[0], raw.at[1], route, kc), ld_sem)
    table_loads = fetch(tables_in, tables, tab_sem)
    loads[2].wait()
    for k in range(5):
        want = jnp.int32(0)
        for t in range(2):
            want = jnp.where(route[t, 0] == k, route[t, 1], want)
        rqs[k] = jnp.full((8, TILE), lax.rem(want - e + ne, ne), jnp.int32)
    for c in range(2):
        loads[c].wait()
        pack(raw.at[c], gath.at[c, 0])
    pl.semaphore_wait(barrier, len(others))

    def copy(src, dst, ssem, rsem, to):
        return pltpu.make_async_remote_copy(
            src_ref=src, dst_ref=dst, send_sem=ssem, recv_sem=rsem, device_id=to, device_id_type=MESH
        )

    chunks = [(c, lo, hi) for c in range(2) for lo, hi in CUTS]
    gathers, answers, asks = [], [], []
    for i, (c, lo, hi) in enumerate(chunks):
        at = pl.ds(lo, hi - lo)
        group = [
            copy(gath.at[c, 0, at], gath.at[c, 4 - k, at], xs.at[i, k], xr.at[i, k], to) for k, to in exposures.items()
        ]
        for one in group:
            one.start()
        gathers.append(group)
        if i == 0:
            for d in (-2, -1, 1, 2):
                k = d + CENTRE
                asks.append(copy(rqs.at[k], rqr.at[k], rs.at[k], rr.at[k], along(d)))
                asks[-1].start()

    def chosen(k, c, lo, hi):
        asked = rqr[k, 0:1, :] if k != CENTRE else rqs[k, 0:1, :]
        asked = jnp.broadcast_to(asked, (hi - lo, TILE))
        value = gath[c, 3, lo:hi]
        for j in (2, 1, 0):
            value = jnp.where(asked == j, gath[c, j, lo:hi], value)
        return value

    def answer(i):
        c, lo, hi = chunks[i]
        at = pl.ds(lo, hi - lo)
        for one in gathers[i]:
            one.wait_recv()
        group = []
        for k in (0, 4, 1, 3):
            ysend[c, k, lo:hi] = chosen(k, c, lo, hi)
            group.append(copy(ysend.at[c, k, at], recv[c].at[k, at], ys.at[i, k], yr.at[i, k], along(CENTRE - k)))
            group[-1].start()
        answers.append(group)

    for one in loads[3:] + table_loads:
        one.wait()
    half = len(CUTS)
    prepare(0, route, kc, pick, pick2, deg, rev, term, prow, alpha, square, toep)
    for one in asks:
        one.wait_recv()
    for i in range(half):
        answer(i)
    prepare(1, route, kc, pick, pick2, deg, rev, term, prow, alpha, square, toep)
    for i in range(half, 2 * half):
        answer(i)
    for c in range(2):
        recv[c][CENTRE] = chosen(CENTRE, c, 0, PACKED)

    for group in answers[:half]:
        for one in group:
            one.wait_recv()
    for t in range(2):
        fill_lhs(recv_flux[route[t, 0]], lhs)
        mix_columns(t, lhs, ca, hbuf, alpha, uh, ul)
    z = jnp.dot(rh[...], uh[...], preferred_element_type=F32)
    z = z[0:128] + z[128:256] + jnp.dot(rh[0:128, :], ul[...], preferred_element_type=F32)
    for t in range(2):
        out[t, 0] = -rows_of(t, route, z)
    for group in answers[half:]:
        for one in group:
            one.wait_recv()
    for t in range(2):
        fill_lhs(recv_var[route[t, 0]], lhs)
        out[t, 1] = variance(t, lhs, toep)
    for one in asks + sum(gathers, []) + sum(answers, []):
        one.wait_send()


def per_device(science_flux, science_var, templ_flux, templ_var, kernel_coefs, tile_route):
    hbm = pl.BlockSpec(memory_space=pl.ANY)
    dma = pltpu.SemaphoreType.DMA
    tables = [jnp.asarray(x) for x in make_tables()]
    n = 2 * len(CUTS)
    delta = pl.pallas_call(
        difference_kernel,
        out_shape=jax.ShapeDtypeStruct((2, 2, TILE, TILE), F32),
        in_specs=[hbm] * (4 + N_TABLES),
        out_specs=pl.BlockSpec(memory_space=pltpu.VMEM),
        scratch_shapes=[
            pltpu.VMEM((2, PAD, PAD), F32),
            pltpu.SMEM((2, 5), jnp.int32),
            pltpu.VMEM((kernel_coefs.shape[1], 1, COLS), F32),
        ]
        + [pltpu.VMEM(x.shape, x.dtype) for x in tables]
        + [
            pltpu.VMEM((2, 4, PACKED, TILE), F32),
            pltpu.VMEM((2, 5, PACKED, TILE), F32),
            pltpu.VMEM((5, PACKED, TILE), F32),
            pltpu.VMEM((5, PACKED, TILE), F32),
            pltpu.VMEM((5, 8, TILE), jnp.int32),
            pltpu.VMEM((5, 8, TILE), jnp.int32),
            pltpu.VMEM((ROWS, 512), BF16),
            pltpu.VMEM((2, 96, TILE), F32),
            pltpu.VMEM((2, 24, TILE), F32),
            pltpu.VMEM((2, 512, 24 * TILE), BF16),
            pltpu.VMEM((ROWS, 1024), F32),
            pltpu.VMEM((8 * ROWS, 768), BF16),
            pltpu.VMEM((8 * ROWS, 768), BF16),
            dma((4,)),
            dma((N_TABLES,)),
            dma((n, 4)),
            dma((n, 4)),
            dma((n, 5)),
            dma((n, 5)),
            dma((5,)),
            dma((5,)),
        ],
        compiler_params=pltpu.CompilerParams(
            collective_id=0, has_side_effects=True, vmem_limit_bytes=63 * 2**20
        ),
        name="difference",
    )(
        templ_flux[0].transpose(1, 0, 2),
        templ_var[0].transpose(1, 0, 2),
        tile_route[0],
        kernel_coefs.transpose(1, 0, 2),
        *tables,
    )
    return jnp.stack([science_flux, science_var], 2) + delta[None]


def solution(mesh):
    return jax.shard_map(
        per_device,
        mesh=mesh,
        in_specs=(
            P("exp", "patch", None, None),
            P("exp", "patch", None, None),
            P("patch", "exp", None, None),
            P("patch", "exp", None, None),
            P("exp", None, None),
            P("exp", "patch", None),
        ),
        out_specs=P("exp", "patch", None, None, None),
        check_vma=False,
    )
```

time: 48.7 us -> 33.7 us (0.69)
  local copies, waits for them, and re-layouts: 9.32 us -> 0.01 us
  Pallas kernels: 38.6 us -> 31.5 us
  other arithmetic: 0 us -> 1.68 us
    unnamed x26 -> x4, local copies, waits for them, and re-layouts: 9.32 us -> 0.01 us
    pallas_call x2 -> x1, Pallas kernels: 38.6 us -> 31.5 us  [per_device(): pl.pallas_call(difference_kernel, out_shape=jax.ShapeDtypeStruct((2, 2, T...]
    add x0 -> x1, other arithmetic: none -> 1.68 us  [per_device(): return jnp.stack([science_flux, science_var], 2) + delta[None]]
where the time goes in v2:
time: 33.7 us; the launch traced here: 33.2 us
  Pallas kernels  31.5 us (93%)
  other arithmetic  1.68 us (5%)
    pallas_call x1, Pallas kernels, per_device(): pl.pallas_call(difference_kernel, out_shape=jax.ShapeDtypeStruct((2, 2, T...  31.5 us
    add x1, other arithmetic, per_device(): return jnp.stack([science_flux, science_var], 2) + delta[None]  1.68 us

profile of v2, /device:TPU:1, one launch (start us, length us, event | category | flops | bytes accessed | tf_op | source)
XLA Modules:
  0.0 33.2 jit_solution(11141628177091549064)
XLA Ops:
  0.0 0.0 copy-start
  0.0 0.0 copy-start.1
  0.0 31.5 %difference.1 = f32[2,2,128,128]{3,2,1,0:T(8,128)} custom-call(f32[150,1,150]{2,1,0:T(1,128)} %bitcast.9, f32[150,1,150]{2,1,0:T(1,128)} %bitcast.10, s32[2,5]{1,0:T(2,128)} %bitcast.13, f32[189,1,192]{2,1,0:T(1,128)} %bitcast.8, bf16[512,1024]{1,0:T(8,128)(2,1)} %constant.16.clone.refs_4_, bf16[256,1280]{1,0:T(8,128)(2,1)} %constant.17.clone.refs_5_, ...), custom_call_target="tpu_custom_call" | custom-call | tf_op jit(solution)/shard_map/difference/pallas_call | solution.py:328
  31.5 0.0 copy-done
  31.5 0.0 copy-done.1
  31.5 1.7 %fusion = f32[1,2,2,128,128]{4,3,2,1,0:T(8,128)} fusion(f32[2,2,128,128]{3,2,1,0:T(8,128)} %difference.1, f32[2,1,128,128]{3,2,1,0:T(8,128)S(1)} %bitcast.11, f32[2,1,128,128]{3,2,1,0:T(8,128)S(1)} %bitcast.12), kind=kLoop, calls=%fused_computation.1 | loop fusion | flops 131072 | bytes 786432 | tf_op jit(solution)/shard_map/add | solution.py:373
Async XLA Ops:
  0.0 31.5 %copy-start = (f32[1,2,128,128]{3,2,1,0:T(8,128)S(1)}, f32[1,2,128,128]{3,2,1,0:T(8,128)}, u32[]{:S(2)}) copy-start(f32[1,2,128,128]{3,2,1,0:T(8,128)} %param.15) | copy-start | bytes 393220
  0.0 31.5 %copy-start.1 = (f32[1,2,128,128]{3,2,1,0:T(8,128)S(1)}, f32[1,2,128,128]{3,2,1,0:T(8,128)}, u32[]{:S(2)}) copy-start(f32[1,2,128,128]{3,2,1,0:T(8,128)} %param.14) | copy-start | bytes 393220

commit v3 on v2

--- a/solution.py
+++ b/solution.py
@@ -24,6 +24,7 @@
 N_TABLES = 8
 CENTRE = 2
 SCALE = TILE * DET_SIDE * 0.5
+DEGREES = 6
 MESH = pl.DeviceIdType.MESH
 BF16 = jnp.bfloat16
 F32 = jnp.float32
@@ -36,18 +37,32 @@
     return hi, lo
 
 
-def make_tables():
-    lags = np.arange(KSIZE) - HALF
-    prof = np.zeros((8, KSIZE))
-    for s in range(2):
-        for m in range(4):
-            ratio = lags / (1.5 + 1.5 * s)
-            row = ratio**m * np.exp(-0.5 * ratio * ratio)
-            prof[s * 4 + m] = row / np.abs(row).sum()
-    toep = np.zeros((8, PAD, TILE))
+def power_profile(s, m):
+    ratio = (np.arange(KSIZE) - HALF) / (1.5 + 1.5 * s)
+    return ratio**m * np.exp(-0.5 * ratio * ratio)
+
+
+def step_up(s, m):
+    return (1.5 + 1.5 * s) * np.abs(power_profile(s, m + 1)).sum() / np.abs(power_profile(s, m)).sum()
+
+
+def banded(profiles):
+    out = np.zeros((len(profiles), PAD, TILE))
     for u in range(KSIZE):
         for x in range(TILE):
-            toep[:, x + u, x] = prof[:, u]
+            out[:, x + u, x] = profiles[:, u]
+    return out
+
+
+def make_tables():
+    prof = np.zeros((8, KSIZE))
+    wide = np.zeros((2 * DEGREES, KSIZE))
+    for s in range(2):
+        for m in range(DEGREES):
+            row = power_profile(s, m)
+            wide[s * DEGREES + m] = row / np.abs(row).sum()
+        prof[s * 4 : s * 4 + 4] = wide[s * DEGREES : s * DEGREES + 4]
+    toep = banded(prof)
     cols = toep.transpose(1, 0, 2).reshape(PAD, 8 * TILE)
     hi, lo = split_np(cols)
     ca = np.zeros((4 * TILE, 8 * TILE), ml_dtypes.bfloat16)
@@ -57,9 +72,9 @@
     ca[384 : 384 + REM] = hi[128:]
     ca[416 : 416 + REM] = hi[128:]
     ca[448 : 448 + REM] = lo[128:]
-    rows = np.zeros((TILE, 8, ROWS))
-    rows[:, :, :PAD] = toep.transpose(2, 0, 1)
-    hi, lo = split_np(rows.reshape(TILE, 8 * ROWS))
+    rows = np.zeros((TILE, 2 * DEGREES, ROWS))
+    rows[:, :, :PAD] = banded(wide).transpose(2, 0, 1)
+    hi, lo = split_np(rows.reshape(TILE, 2 * DEGREES * ROWS))
     rh = np.concatenate([hi, lo], 0)
     xdeg = [0, 1, 0, 2, 1, 0]
     ydeg = [0, 0, 1, 0, 1, 2]
@@ -83,21 +98,27 @@
     return ca, rh, pick, pick2, deg, rev, term, prow
 
 
-def fill_lhs(src, dst):
-    main = src[0:MAIN]
-    main = jnp.concatenate([main, jnp.zeros((ROWS - MAIN, TILE), F32)], 0)
-    hi = main.astype(BF16)
-    dst[:, 0:128] = hi
-    dst[:, 128:256] = (main - hi.astype(F32)).astype(BF16)
-    dst[:, 256:384] = hi
-    other = src[MAIN:PACKED]
+def fill_lhs(tiles, dst):
     lane = lax.broadcasted_iota(jnp.int32, (32, TILE), 1)
-    for g in range(GROUPS):
-        part = pltpu.roll(other, TILE - REM * g, 1) if g else other
-        part = jnp.where(lane < REM, part, 0.0)
-        hi = part.astype(BF16).astype(F32)
-        part = hi + pltpu.roll(part - hi, 32, 1) + pltpu.roll(hi, 64, 1)
-        dst[32 * g : 32 * g + 32, 384:512] = part.astype(BF16)
+    pieces = []
+    for src in tiles:
+        main = jnp.concatenate([src[0:MAIN], jnp.zeros((ROWS - MAIN, TILE), F32)], 0)
+        hi = main.astype(BF16)
+        lo = (main - hi.astype(F32)).astype(BF16)
+        other = src[MAIN:PACKED]
+        parts = []
+        for g in range(GROUPS):
+            part = pltpu.roll(other, TILE - REM * g, 1) if g else other
+            part = jnp.where(lane < REM, part, 0.0)
+            top = part.astype(BF16).astype(F32)
+            parts.append((top + pltpu.roll(part - top, 32, 1) + pltpu.roll(top, 64, 1)).astype(BF16))
+        pieces.append((hi, lo, jnp.concatenate(parts, 0)))
+    for t, (hi, lo, rest) in enumerate(pieces):
+        at = slice(t * ROWS, (t + 1) * ROWS)
+        dst[at, 0:128] = hi
+        dst[at, 128:256] = lo
+        dst[at, 256:384] = hi
+        dst[at, 384:512] = rest
 
 
 def prepare(t, route, kc, pick, pick2, deg, rev, term, prow, alpha, square, toep):
@@ -142,21 +163,40 @@
     lax.fori_loop(0, KSIZE, lag, 0)
 
 
-def mix_columns(t, lhs, ca, hbuf, alpha, uh, ul):
-    hbuf[...] = jnp.dot(lhs[...], ca[...], preferred_element_type=F32)
-
+def mix_columns(route, hbuf, alpha, uh, ul):
     def chunk(i, carry):
-        at = pl.ds(pl.multiple_of(i * 16, 16), 16)
-        for s in range(2):
-            parts = [hbuf[at, (s * 4 + my) * TILE : (s * 4 + my + 1) * TILE] for my in range(4)]
-            for mx in range(4):
-                for j in range(3):
-                    first = ((s * 4 + mx) * 3 + j) * 4
-                    total = alpha[t, first : first + 1, :] * parts[0]
-                    for my in range(1, 4):
-                        total = total + alpha[t, first + my : first + my + 1, :] * parts[my]
-                    to = pl.ds(pl.multiple_of((s * 4 + mx) * ROWS + i * 16, 16), 16)
-                    cols = slice((t * 3 + j) * TILE, (t * 3 + j + 1) * TILE)
+        subs = lax.broadcasted_iota(jnp.int32, (16, TILE), 0).astype(F32)
+        for t in range(2):
+            first_row = route[t, 2].astype(F32) * TILE + (i * 16).astype(F32) + (0.5 - HALF)
+            yc = (subs + first_row) / SCALE - 1.0
+            at = pl.ds(pl.multiple_of(t * ROWS + i * 16, 16), 16)
+            for s in range(2):
+                parts = [hbuf[at, (s * 4 + my) * TILE : (s * 4 + my + 1) * TILE] for my in range(4)]
+                mixed = []
+                for mx in range(4):
+                    terms = []
+                    for j in range(3):
+                        first = ((s * 4 + mx) * 3 + j) * 4
+                        total = alpha[t, first : first + 1, :] * parts[0]
+                        for my in range(1, 4):
+                            total = total + alpha[t, first + my : first + my + 1, :] * parts[my]
+                        terms.append(total)
+                    mixed.append(terms)
+                for m in range(DEGREES):
+                    total = None
+                    if m < 4:
+                        a, b, c = mixed[m]
+                        total = a + yc * (b + yc * c)
+                    if 1 <= m <= 4:
+                        a, b, c = mixed[m - 1]
+                        term = (b + (2.0 * yc) * c) * np.float32(-step_up(s, m - 1) / SCALE)
+                        total = term if total is None else total + term
+                    if m >= 2:
+                        a, b, c = mixed[m - 2]
+                        term = c * np.float32(step_up(s, m - 2) * step_up(s, m - 1) / SCALE**2)
+                        total = term if total is None else total + term
+                    to = pl.ds(pl.multiple_of((s * DEGREES + m) * ROWS + i * 16, 16), 16)
+                    cols = slice(t * TILE, (t + 1) * TILE)
                     hi = total.astype(BF16)
                     uh[to, cols] = hi
                     ul[to, cols] = (total - hi.astype(F32)).astype(BF16)
@@ -165,23 +205,19 @@
     lax.fori_loop(0, ROWS // 16, chunk, 0)
 
 
-def rows_of(t, route, z):
-    row = route[t, 2].astype(F32)
-    subs = lax.broadcasted_iota(jnp.int32, (TILE, TILE), 0).astype(F32)
-    ys = (row * TILE + subs + 0.5) / SCALE - 1.0
-    z = z[:, t * 384 : (t + 1) * 384]
-    return z[:, 0:128] + ys * (z[:, 128:256] + ys * z[:, 256:384])
-
-
 def variance(t, lhs, toep):
     acc = jnp.zeros((TILE, TILE), F32)
-    for r in range(8):
-        width = 384 if r < 7 else 256
-        part = jnp.dot(lhs[...], toep[t, :, r * 384 : r * 384 + width], preferred_element_type=F32)
-        total = part[0:136, 0:128] + part[8:144, 128:256]
-        if width == 384:
-            total = total + part[16:152, 256:384]
-        acc = acc + total[r : r + TILE]
+    for r in range(0, 8, 2):
+        width = 768 if r < 6 else 640
+        part = jnp.dot(
+            lhs[t * ROWS : (t + 1) * ROWS, :], toep[t, :, r * 384 : r * 384 + width], preferred_element_type=F32
+        )
+        for k in range(2):
+            at = k * 384
+            total = part[0:136, at : at + 128] + part[8:144, at + 128 : at + 256]
+            if at + 384 <= width:
+                total = total + part[16:152, at + 256 : at + 384]
+            acc = acc + total[r + k : r + k + TILE]
     return acc
 
 
@@ -210,12 +246,12 @@
 
 def difference_kernel(*refs):
     n = N_TABLES
-    tf, tv, route_in, kc_in = refs[:4]
-    tables_in, out = refs[4 : 4 + n], refs[4 + n]
-    raw, route, kc = refs[5 + n : 8 + n]
-    tables = refs[8 + n : 8 + 2 * n]
-    gath, ysend, recv_flux, recv_var, rqs, rqr, lhs, alpha, square, toep, hbuf, uh, ul = refs[8 + 2 * n : 21 + 2 * n]
-    ld_sem, tab_sem, xs, xr, ys, yr, rs, rr = refs[21 + 2 * n :]
+    tf, tv, route_in, kc_in, sf_in, sv_in = refs[:6]
+    tables_in, out = refs[6 : 6 + n], refs[6 + n]
+    raw, route, kc, sci, result = refs[7 + n : 12 + n]
+    tables = refs[12 + n : 12 + 2 * n]
+    gath, ysend, recv_flux, recv_var, rqs, rqr, lhs, alpha, square, toep, hbuf, uh, ul = refs[12 + 2 * n : 25 + 2 * n]
+    ld_sem, tab_sem, out_sem, xs, xr, ys, yr, rs, rr = refs[25 + 2 * n :]
     recv = (recv_flux, recv_var)
     ca, rh, pick, pick2, deg, rev, term, prow = tables
 
@@ -232,7 +268,11 @@
     others = list(exposures.values()) + [along(d) for d in (-2, -1, 1, 2)]
     for other in others:
         pl.semaphore_signal(barrier, inc=1, device_id=other, device_id_type=MESH)
-    loads = fetch((tf.at[:, 0, :], tv.at[:, 0, :], route_in, kc_in), (raw.at[0], raw.at[1], route, kc), ld_sem)
+    loads = fetch(
+        (tf.at[:, 0, :], tv.at[:, 0, :], route_in, kc_in, sf_in, sv_in),
+        (raw.at[0], raw.at[1], route, kc, sci.at[0], sci.at[1]),
+        ld_sem,
+    )
     table_loads = fetch(tables_in, tables, tab_sem)
     loads[2].wait()
     for k in range(5):
@@ -303,19 +343,28 @@
     for group in answers[:half]:
         for one in group:
             one.wait_recv()
-    for t in range(2):
-        fill_lhs(recv_flux[route[t, 0]], lhs)
-        mix_columns(t, lhs, ca, hbuf, alpha, uh, ul)
+    fill_lhs([recv_flux[route[t, 0]] for t in range(2)], lhs)
+    hbuf[...] = jnp.dot(lhs[...], ca[...], preferred_element_type=F32)
+    mix_columns(route, hbuf, alpha, uh, ul)
     z = jnp.dot(rh[...], uh[...], preferred_element_type=F32)
     z = z[0:128] + z[128:256] + jnp.dot(rh[0:128, :], ul[...], preferred_element_type=F32)
+    stores = []
+
+    def keep(c, t, value):
+        result[c, t] = value
+        stores.append(pltpu.make_async_copy(result.at[c, t], out.at[t, c], out_sem.at[c, t]))
+        stores[-1].start()
+
     for t in range(2):
-        out[t, 0] = -rows_of(t, route, z)
+        keep(0, t, sci[0, t] - z[:, t * TILE : (t + 1) * TILE])
     for group in answers[half:]:
         for one in group:
             one.wait_recv()
+    fill_lhs([recv_var[route[t, 0]] for t in range(2)], lhs)
     for t in range(2):
-        fill_lhs(recv_var[route[t, 0]], lhs)
-        out[t, 1] = variance(t, lhs, toep)
+        keep(1, t, sci[1, t] + variance(t, lhs, toep))
+    for one in stores:
+        one.wait()
     for one in asks + sum(gathers, []) + sum(answers, []):
         one.wait_send()
 
@@ -325,15 +374,17 @@
     dma = pltpu.SemaphoreType.DMA
     tables = [jnp.asarray(x) for x in make_tables()]
     n = 2 * len(CUTS)
-    delta = pl.pallas_call(
+    out = pl.pallas_call(
         difference_kernel,
         out_shape=jax.ShapeDtypeStruct((2, 2, TILE, TILE), F32),
-        in_specs=[hbm] * (4 + N_TABLES),
-        out_specs=pl.BlockSpec(memory_space=pltpu.VMEM),
+        in_specs=[hbm] * (6 + N_TABLES),
+        out_specs=hbm,
         scratch_shapes=[
             pltpu.VMEM((2, PAD, PAD), F32),
             pltpu.SMEM((2, 5), jnp.int32),
             pltpu.VMEM((kernel_coefs.shape[1], 1, COLS), F32),
+            pltpu.VMEM((2, 2, TILE, TILE), F32),
+            pltpu.VMEM((2, 2, TILE, TILE), F32),
         ]
         + [pltpu.VMEM(x.shape, x.dtype) for x in tables]
         + [
@@ -343,15 +394,16 @@
             pltpu.VMEM((5, PACKED, TILE), F32),
             pltpu.VMEM((5, 8, TILE), jnp.int32),
             pltpu.VMEM((5, 8, TILE), jnp.int32),
-            pltpu.VMEM((ROWS, 512), BF16),
+            pltpu.VMEM((2 * ROWS, 512), BF16),
             pltpu.VMEM((2, 96, TILE), F32),
             pltpu.VMEM((2, 24, TILE), F32),
             pltpu.VMEM((2, 512, 24 * TILE), BF16),
-            pltpu.VMEM((ROWS, 1024), F32),
-            pltpu.VMEM((8 * ROWS, 768), BF16),
-            pltpu.VMEM((8 * ROWS, 768), BF16),
-            dma((4,)),
+            pltpu.VMEM((2 * ROWS, 1024), F32),
+            pltpu.VMEM((2 * DEGREES * ROWS, 256), BF16),
+            pltpu.VMEM((2 * DEGREES * ROWS, 256), BF16),
+            dma((6,)),
             dma((N_TABLES,)),
+            dma((2, 2)),
             dma((n, 4)),
             dma((n, 4)),
             dma((n, 5)),
@@ -368,9 +420,11 @@
         templ_var[0].transpose(1, 0, 2),
         tile_route[0],
         kernel_coefs.transpose(1, 0, 2),
+        science_flux[0],
+        science_var[0],
         *tables,
     )
-    return jnp.stack([science_flux, science_var], 2) + delta[None]
+    return out[None]
 
 
 def solution(mesh):

time: 33.7 us -> 33 us (0.979)
  other arithmetic: 1.68 us -> 0 us
  local copies, waits for them, and re-layouts: 0.01 us -> 1.67 us
  Pallas kernels: 31.5 us -> 30.8 us
    add x1 -> x0, other arithmetic: 1.68 us -> none  [per_device(): return jnp.stack([science_flux, science_var], 2) + delta[None]]
    unnamed x4 -> x1, local copies, waits for them, and re-layouts: 0.01 us -> 1.67 us
    pallas_call x1, Pallas kernels: 31.5 us -> 30.8 us  [per_device(): pl.pallas_call(difference_kernel, out_shape=jax.ShapeDtypeStruct((2, 2, T...]
where the time goes in v3:
time: 33 us; the launch traced here: 32.5 us
  Pallas kernels  30.8 us (93%)
  local copies, waits for them, and re-layouts  1.67 us (5%)
    pallas_call x1, Pallas kernels, per_device(): pl.pallas_call(difference_kernel, out_shape=jax.ShapeDtypeStruct((2, 2, T...  30.8 us
    unnamed x1, local copies, waits for them, and re-layouts  1.67 us

profile of v3, /device:TPU:1, one launch (start us, length us, event | category | flops | bytes accessed | tf_op | source)
XLA Modules:
  0.0 32.5 jit_solution(4240789152891701341)
XLA Ops:
  0.0 30.8 %difference.1 = f32[2,2,128,128]{3,2,1,0:T(8,128)} custom-call(f32[150,1,150]{2,1,0:T(1,128)} %bitcast.9, f32[150,1,150]{2,1,0:T(1,128)} %bitcast.10, s32[2,5]{1,0:T(2,128)} %bitcast.13, f32[189,1,192]{2,1,0:T(1,128)} %bitcast.8, f32[2,128,128]{2,1,0:T(8,128)} %bitcast.11, f32[2,128,128]{2,1,0:T(8,128)} %bitcast.12, ...), custom_call_target="tpu_custom_call" | custom-call | tf_op jit(solution)/shard_map/difference/pallas_call | solution.py:377
  30.9 1.7 %copy.16 = f32[1,2,2,128,128]{4,3,2,1,0:T(8,128)} copy(f32[1,2,2,128,128]{4,3,2,1,0:T(8,128)} %bitcast.7) | data formatting | bytes 524288

commit v4 on v3

--- a/solution.py
+++ b/solution.py
@@ -128,7 +128,8 @@
     lanes = lax.broadcasted_iota(jnp.int32, (1, TILE), 1).astype(F32)
     xs = (col * TILE + lanes + 0.5) / SCALE - 1.0
     powers = jnp.where(deg[...] == 0.0, 1.0, jnp.where(deg[...] == 1.0, xs, xs * xs))
-    alpha[t] = jnp.dot(pick[...] * coefs, powers, precision=HIGH, preferred_element_type=F32)
+    rows = jnp.dot(pick[...] * coefs, powers, precision=HIGH, preferred_element_type=F32)
+    alpha[t] = jnp.broadcast_to(rows[:, None, :], (96, 8, TILE))
     cx = (col * TILE + TILE * 0.5) / SCALE - 1.0
     cy = (row * TILE + TILE * 0.5) / SCALE - 1.0
     kinds = term[...]
@@ -163,39 +164,49 @@
     lax.fori_loop(0, KSIZE, lag, 0)
 
 
-def mix_columns(route, hbuf, alpha, uh, ul):
+def fill_maps(t, route, alpha, maps):
+    subs = lax.broadcasted_iota(jnp.int32, (8, TILE), 0).astype(F32)
+    row = route[t, 2].astype(F32) * TILE + (0.5 - HALF)
+
     def chunk(i, carry):
-        subs = lax.broadcasted_iota(jnp.int32, (16, TILE), 0).astype(F32)
-        for t in range(2):
-            first_row = route[t, 2].astype(F32) * TILE + (i * 16).astype(F32) + (0.5 - HALF)
-            yc = (subs + first_row) / SCALE - 1.0
-            at = pl.ds(pl.multiple_of(t * ROWS + i * 16, 16), 16)
-            for s in range(2):
-                parts = [hbuf[at, (s * 4 + my) * TILE : (s * 4 + my + 1) * TILE] for my in range(4)]
-                mixed = []
-                for mx in range(4):
-                    terms = []
-                    for j in range(3):
-                        first = ((s * 4 + mx) * 3 + j) * 4
-                        total = alpha[t, first : first + 1, :] * parts[0]
-                        for my in range(1, 4):
-                            total = total + alpha[t, first + my : first + my + 1, :] * parts[my]
-                        terms.append(total)
-                    mixed.append(terms)
+        yc = (subs + (row + (i * 8).astype(F32))) / SCALE - 1.0
+        twice = 2.0 * yc
+        at = pl.ds(pl.multiple_of(i * 8, 8), 8)
+        for s in range(2):
+            for my in range(4):
+                abc = [[alpha[t, ((s * 4 + mx) * 3 + j) * 4 + my] for j in range(3)] for mx in range(4)]
                 for m in range(DEGREES):
                     total = None
                     if m < 4:
-                        a, b, c = mixed[m]
+                        a, b, c = abc[m]
                         total = a + yc * (b + yc * c)
                     if 1 <= m <= 4:
-                        a, b, c = mixed[m - 1]
-                        term = (b + (2.0 * yc) * c) * np.float32(-step_up(s, m - 1) / SCALE)
+                        a, b, c = abc[m - 1]
+                        term = (b + twice * c) * np.float32(-step_up(s, m - 1) / SCALE)
                         total = term if total is None else total + term
                     if m >= 2:
-                        a, b, c = mixed[m - 2]
+                        a, b, c = abc[m - 2]
                         term = c * np.float32(step_up(s, m - 2) * step_up(s, m - 1) / SCALE**2)
                         total = term if total is None else total + term
-                    to = pl.ds(pl.multiple_of((s * DEGREES + m) * ROWS + i * 16, 16), 16)
+                    maps[t, s * DEGREES + m, my, at, :] = total
+        return carry
+
+    lax.fori_loop(0, ROWS // 8, chunk, 0)
+
+
+def mix_columns(hbuf, maps, uh, ul):
+    def chunk(i, carry):
+        at = pl.ds(pl.multiple_of(i * 16, 16), 16)
+        for t in range(2):
+            here = pl.ds(pl.multiple_of(t * ROWS + i * 16, 16), 16)
+            for s in range(2):
+                parts = [hbuf[here, (s * 4 + my) * TILE : (s * 4 + my + 1) * TILE] for my in range(4)]
+                for m in range(DEGREES):
+                    q = s * DEGREES + m
+                    total = maps[t, q, 0, at, :] * parts[0]
+                    for my in range(1, 4):
+                        total = total + maps[t, q, my, at, :] * parts[my]
+                    to = pl.ds(pl.multiple_of(q * ROWS + i * 16, 16), 16)
                     cols = slice(t * TILE, (t + 1) * TILE)
                     hi = total.astype(BF16)
                     uh[to, cols] = hi
@@ -250,8 +261,8 @@
     tables_in, out = refs[6 : 6 + n], refs[6 + n]
     raw, route, kc, sci, result = refs[7 + n : 12 + n]
     tables = refs[12 + n : 12 + 2 * n]
-    gath, ysend, recv_flux, recv_var, rqs, rqr, lhs, alpha, square, toep, hbuf, uh, ul = refs[12 + 2 * n : 25 + 2 * n]
-    ld_sem, tab_sem, out_sem, xs, xr, ys, yr, rs, rr = refs[25 + 2 * n :]
+    gath, ysend, recv_flux, recv_var, rqs, rqr, lhs, alpha, maps, square, toep, hbuf, uh, ul = refs[12 + 2 * n : 26 + 2 * n]
+    ld_sem, tab_sem, out_sem, xs, xr, ys, yr, rs, rr = refs[26 + 2 * n :]
     recv = (recv_flux, recv_var)
     ca, rh, pick, pick2, deg, rev, term, prow = tables
 
@@ -329,14 +340,27 @@
     for one in loads[3:] + table_loads:
         one.wait()
     half = len(CUTS)
-    prepare(0, route, kc, pick, pick2, deg, rev, term, prow, alpha, square, toep)
+    for t in range(2):
+        prepare(t, route, kc, pick, pick2, deg, rev, term, prow, alpha, square, toep)
     for one in asks:
         one.wait_recv()
     for i in range(half):
         answer(i)
-    prepare(1, route, kc, pick, pick2, deg, rev, term, prow, alpha, square, toep)
+    last = p >= npatch - 2
+
+    @pl.when(jnp.logical_not(last))
+    def _():
+        for t in range(2):
+            fill_maps(t, route, alpha, maps)
+
     for i in range(half, 2 * half):
         answer(i)
+
+    @pl.when(last)
+    def _():
+        for t in range(2):
+            fill_maps(t, route, alpha, maps)
+
     for c in range(2):
         recv[c][CENTRE] = chosen(CENTRE, c, 0, PACKED)
 
@@ -345,7 +369,7 @@
             one.wait_recv()
     fill_lhs([recv_flux[route[t, 0]] for t in range(2)], lhs)
     hbuf[...] = jnp.dot(lhs[...], ca[...], preferred_element_type=F32)
-    mix_columns(route, hbuf, alpha, uh, ul)
+    mix_columns(hbuf, maps, uh, ul)
     z = jnp.dot(rh[...], uh[...], preferred_element_type=F32)
     z = z[0:128] + z[128:256] + jnp.dot(rh[0:128, :], ul[...], preferred_element_type=F32)
     stores = []
@@ -395,7 +419,8 @@
             pltpu.VMEM((5, 8, TILE), jnp.int32),
             pltpu.VMEM((5, 8, TILE), jnp.int32),
             pltpu.VMEM((2 * ROWS, 512), BF16),
-            pltpu.VMEM((2, 96, TILE), F32),
+            pltpu.VMEM((2, 96, 8, TILE), F32),
+            pltpu.VMEM((2, 2 * DEGREES, 4, ROWS, TILE), F32),
             pltpu.VMEM((2, 24, TILE), F32),
             pltpu.VMEM((2, 512, 24 * TILE), BF16),
             pltpu.VMEM((2 * ROWS, 1024), F32),

time: 33 us -> 32.9 us (level)
  no operation moved by 1% of the time
where the time goes in v4:
time: 32.9 us; the launch traced here: 32.7 us
  Pallas kernels  31.1 us (95%)
  local copies, waits for them, and re-layouts  1.67 us (5%)
    pallas_call x1, Pallas kernels, per_device(): pl.pallas_call(difference_kernel, out_shape=jax.ShapeDtypeStruct((2, 2, T...  31.1 us
    unnamed x1, local copies, waits for them, and re-layouts  1.67 us

profile of v4, /device:TPU:1, one launch (start us, length us, event | category | flops | bytes accessed | tf_op | source)
XLA Modules:
  0.0 32.7 jit_solution(8135221565628259455)
XLA Ops:
  0.0 31.1 %difference.1 = f32[2,2,128,128]{3,2,1,0:T(8,128)} custom-call(f32[150,1,150]{2,1,0:T(1,128)} %bitcast.9, f32[150,1,150]{2,1,0:T(1,128)} %bitcast.10, s32[2,5]{1,0:T(2,128)} %bitcast.13, f32[189,1,192]{2,1,0:T(1,128)} %bitcast.8, f32[2,128,128]{2,1,0:T(8,128)} %bitcast.11, f32[2,128,128]{2,1,0:T(8,128)} %bitcast.12, ...), custom_call_target="tpu_custom_call" | custom-call | tf_op jit(solution)/shard_map/difference/pallas_call | solution.py:401
  31.1 1.7 %copy.16 = f32[1,2,2,128,128]{4,3,2,1,0:T(8,128)} copy(f32[1,2,2,128,128]{4,3,2,1,0:T(8,128)} %bitcast.7) | data formatting | bytes 524288

commit v5 on v4

--- a/solution.py
+++ b/solution.py
@@ -340,13 +340,20 @@
     for one in loads[3:] + table_loads:
         one.wait()
     half = len(CUTS)
-    for t in range(2):
+    last = p >= npatch - 2
+
+    def ready(t, carry):
         prepare(t, route, kc, pick, pick2, deg, rev, term, prow, alpha, square, toep)
+        return carry
+
+    @pl.when(jnp.logical_not(last))
+    def _():
+        lax.fori_loop(0, 2, ready, 0)
+
     for one in asks:
         one.wait_recv()
     for i in range(half):
         answer(i)
-    last = p >= npatch - 2
 
     @pl.when(jnp.logical_not(last))
     def _():
@@ -358,6 +365,7 @@
 
     @pl.when(last)
     def _():
+        lax.fori_loop(0, 2, ready, 0)
         for t in range(2):
             fill_maps(t, route, alpha, maps)
 

time: 32.9 us -> 32.1 us (0.976); the launches traced: 32.7 us -> 31.5 us
  Pallas kernels: 31.1 us -> 29.9 us
    pallas_call x1, Pallas kernels: 31.1 us -> 29.9 us  [per_device(): pl.pallas_call(difference_kernel, out_shape=jax.ShapeDtypeStruct((2, 2, T...]
where the time goes in v5:
time: 32.1 us; the launch traced here: 31.5 us
  Pallas kernels  29.9 us (93%)
  local copies, waits for them, and re-layouts  1.67 us (5%)
    pallas_call x1, Pallas kernels, per_device(): pl.pallas_call(difference_kernel, out_shape=jax.ShapeDtypeStruct((2, 2, T...  29.9 us
    unnamed x1, local copies, waits for them, and re-layouts  1.67 us

profile of v5, /device:TPU:1, one launch (start us, length us, event | category | flops | bytes accessed | tf_op | source)
XLA Modules:
  0.0 31.5 jit_solution(1353332367316180556)
XLA Ops:
  0.0 29.9 %difference.1 = f32[2,2,128,128]{3,2,1,0:T(8,128)} custom-call(f32[150,1,150]{2,1,0:T(1,128)} %bitcast.9, f32[150,1,150]{2,1,0:T(1,128)} %bitcast.10, s32[2,5]{1,0:T(2,128)} %bitcast.13, f32[189,1,192]{2,1,0:T(1,128)} %bitcast.8, f32[2,128,128]{2,1,0:T(8,128)} %bitcast.11, f32[2,128,128]{2,1,0:T(8,128)} %bitcast.12, ...), custom_call_target="tpu_custom_call" | custom-call | tf_op jit(solution)/shard_map/difference/pallas_call | solution.py:409
  29.9 1.7 %copy.16 = f32[1,2,2,128,128]{4,3,2,1,0:T(8,128)} copy(f32[1,2,2,128,128]{4,3,2,1,0:T(8,128)} %bitcast.7) | data formatting | bytes 524288

commit v6 on v5

--- a/solution.py
+++ b/solution.py
@@ -21,7 +21,8 @@
 GROUPS = 5
 ROWS = 160
 CUTS = ((0, 96), (96, PACKED))
-N_TABLES = 8
+N_TABLES = 3
+VMEM_LIMIT = 54912 * 2**10
 CENTRE = 2
 SCALE = TILE * DET_SIDE * 0.5
 DEGREES = 6
@@ -95,7 +96,14 @@
                 rev[col, -v % TILE] = prof[s * 4 + my, v]
     prow = np.zeros((24, 8), np.float32)
     prow[:KSIZE] = prof.T
-    return ca, rh, pick, pick2, deg, rev, term, prow
+    tab = np.zeros((328, 256), np.float32)
+    tab[0:96, :COLS] = pick
+    tab[96:104, :COLS] = pick2
+    tab[104:112, :COLS] = term
+    tab[112:304, 0:128] = deg
+    tab[112:304, 128:256] = rev
+    tab[304:328, 0:8] = prow
+    return ca, rh, tab
 
 
 def fill_lhs(tiles, dst):
@@ -258,13 +266,16 @@
 def difference_kernel(*refs):
     n = N_TABLES
     tf, tv, route_in, kc_in, sf_in, sv_in = refs[:6]
-    tables_in, out = refs[6 : 6 + n], refs[6 + n]
-    raw, route, kc, sci, result = refs[7 + n : 12 + n]
-    tables = refs[12 + n : 12 + 2 * n]
-    gath, ysend, recv_flux, recv_var, rqs, rqr, lhs, alpha, maps, square, toep, hbuf, uh, ul = refs[12 + 2 * n : 26 + 2 * n]
-    ld_sem, tab_sem, out_sem, xs, xr, ys, yr, rs, rr = refs[26 + 2 * n :]
+    tables_in, outs = refs[6 : 6 + n], refs[6 + n : 10 + n]
+    raw, route, kc, sci = refs[10 + n : 14 + n]
+    tables = refs[14 + n : 14 + 2 * n]
+    gath, ysend, recv_flux, recv_var, rqs, rqr, lhs, alpha, maps, square, toep, hbuf, uh, ul = refs[14 + 2 * n : 28 + 2 * n]
+    ld_sem, tab_sem, xs, xr, ys, yr, rs, rr = refs[28 + 2 * n :]
     recv = (recv_flux, recv_var)
-    ca, rh, pick, pick2, deg, rev, term, prow = tables
+    ca, rh, tab = tables
+    pick, pick2, term = (tab.at[lo:hi, 0:COLS] for lo, hi in ((0, 96), (96, 104), (104, 112)))
+    deg, rev = tab.at[112:304, 0:128], tab.at[112:304, 128:256]
+    prow = tab.at[304:328, 0:8]
 
     e = lax.axis_index("exp")
     p = lax.axis_index("patch")
@@ -380,23 +391,14 @@
     mix_columns(hbuf, maps, uh, ul)
     z = jnp.dot(rh[...], uh[...], preferred_element_type=F32)
     z = z[0:128] + z[128:256] + jnp.dot(rh[0:128, :], ul[...], preferred_element_type=F32)
-    stores = []
-
-    def keep(c, t, value):
-        result[c, t] = value
-        stores.append(pltpu.make_async_copy(result.at[c, t], out.at[t, c], out_sem.at[c, t]))
-        stores[-1].start()
-
     for t in range(2):
-        keep(0, t, sci[0, t] - z[:, t * TILE : (t + 1) * TILE])
+        outs[2 * t][...] = sci[0, t] - z[:, t * TILE : (t + 1) * TILE]
     for group in answers[half:]:
         for one in group:
             one.wait_recv()
     fill_lhs([recv_var[route[t, 0]] for t in range(2)], lhs)
     for t in range(2):
-        keep(1, t, sci[1, t] + variance(t, lhs, toep))
-    for one in stores:
-        one.wait()
+        outs[2 * t + 1][...] = sci[1, t] + variance(t, lhs, toep)
     for one in asks + sum(gathers, []) + sum(answers, []):
         one.wait_send()
 
@@ -408,14 +410,13 @@
     n = 2 * len(CUTS)
     out = pl.pallas_call(
         difference_kernel,
-        out_shape=jax.ShapeDtypeStruct((2, 2, TILE, TILE), F32),
+        out_shape=(jax.ShapeDtypeStruct((TILE, TILE), F32),) * 4,
         in_specs=[hbm] * (6 + N_TABLES),
-        out_specs=hbm,
+        out_specs=(pl.BlockSpec(memory_space=pltpu.VMEM),) * 4,
         scratch_shapes=[
             pltpu.VMEM((2, PAD, PAD), F32),
             pltpu.SMEM((2, 5), jnp.int32),
             pltpu.VMEM((kernel_coefs.shape[1], 1, COLS), F32),
-            pltpu.VMEM((2, 2, TILE, TILE), F32),
             pltpu.VMEM((2, 2, TILE, TILE), F32),
         ]
         + [pltpu.VMEM(x.shape, x.dtype) for x in tables]
@@ -436,7 +437,6 @@
             pltpu.VMEM((2 * DEGREES * ROWS, 256), BF16),
             dma((6,)),
             dma((N_TABLES,)),
-            dma((2, 2)),
             dma((n, 4)),
             dma((n, 4)),
             dma((n, 5)),
@@ -445,7 +445,7 @@
             dma((5,)),
         ],
         compiler_params=pltpu.CompilerParams(
-            collective_id=0, has_side_effects=True, vmem_limit_bytes=63 * 2**20
+            collective_id=0, has_side_effects=True, vmem_limit_bytes=VMEM_LIMIT
         ),
         name="difference",
     )(
@@ -457,7 +457,7 @@
         science_var[0],
         *tables,
     )
-    return out[None]
+    return jnp.stack(out).reshape(1, 2, 2, TILE, TILE)
 
 
 def solution(mesh):

time: 32.1 us -> 31.1 us (0.969)
  local copies, waits for them, and re-layouts: 1.67 us -> 0.68 us
  Pallas kernels: 29.9 us -> 29.1 us
  other arithmetic: 0 us -> 0.72 us
    unnamed x1 -> x2, local copies, waits for them, and re-layouts: 1.67 us -> 0.68 us
    another operation x0 -> x1, other arithmetic: none -> 0.72 us  [per_device(): return jnp.stack(out).reshape(1, 2, 2, TILE, TILE)]
    pallas_call x1, Pallas kernels: 29.9 us -> 29.1 us  [per_device(): pl.pallas_call(difference_kernel, out_shape=(jax.ShapeDtypeStruct((TILE,...]
where the time goes in v6:
time: 31.1 us; the launch traced here: 30.5 us
  Pallas kernels  29.1 us (94%)
  other arithmetic  0.72 us (2%)
  local copies, waits for them, and re-layouts  0.68 us (2%)
    pallas_call x1, Pallas kernels, per_device(): pl.pallas_call(difference_kernel, out_shape=(jax.ShapeDtypeStruct((TILE,...  29.1 us
    another operation x1, other arithmetic, per_device(): return jnp.stack(out).reshape(1, 2, 2, TILE, TILE)  0.72 us
    unnamed x2, local copies, waits for them, and re-layouts  0.68 us

profile of v6, /device:TPU:1, one launch (start us, length us, event | category | flops | bytes accessed | tf_op | source)
XLA Modules:
  0.0 30.5 jit_solution(15121190193128887756)
XLA Ops:
  0.0 0.0 copy-start
  0.0 0.7 %copy-done = s32[1,2,5]{2,1,0:T(2,128)S(1)} copy-done((s32[1,2,5]{2,1,0:T(2,128)S(1)}, s32[1,2,5]{2,1,0:T(2,128)}, u32[]{:S(2)}) %copy-start) | copy-done | bytes 64
  0.7 29.1 %difference.1 = (f32[128,128]{1,0:T(8,128)S(1)}, f32[128,128]{1,0:T(8,128)S(1)}, f32[128,128]{1,0:T(8,128)S(1)}, f32[128,128]{1,0:T(8,128)S(1)}) custom-call(f32[150,1,150]{2,1,0:T(1,128)} %bitcast.17, f32[150,1,150]{2,1,0:T(1,128)} %bitcast.18, s32[2,5]{1,0:T(2,128)S(1)} %bitcast.15, f32[189,1,192]{2,1,0:T(1,128)} %bitcast.16, f32[2,128,128]{2,1,0:T(8,128)} %bitcast.19, ...), custom_call_target="tpu_custom_call" | custom-call | tf_op jit(solution)/shard_map/difference/pallas_call | solution.py:411
  29.8 0.7 %pad_maximum_fusion = f32[4,128,128]{2,1,0:T(8,128)} fusion(f32[1,128,128]{2,1,0:T(8,128)S(1)} %bitcast.14, f32[1,128,128]{2,1,0:T(8,128)S(1)} %bitcast.13, f32[1,128,128]{2,1,0:T(8,128)S(1)} %bitcast.12, f32[1,128,128]{2,1,0:T(8,128)S(1)} %bitcast.11), kind=kLoop, calls=%fused_computation | loop fusion | flops 196608 | bytes 524288 | tf_op jit(solution)/shard_map/stack | solution.py:460
Async XLA Ops:
  0.0 0.7 %copy-start = (s32[1,2,5]{2,1,0:T(2,128)S(1)}, s32[1,2,5]{2,1,0:T(2,128)}, u32[]{:S(2)}) copy-start(s32[1,2,5]{2,1,0:T(2,128)} %param.14) | copy-start | bytes 124

commit v7 on v6

--- a/solution.py
+++ b/solution.py
@@ -265,12 +265,12 @@
 
 def difference_kernel(*refs):
     n = N_TABLES
-    tf, tv, route_in, kc_in, sf_in, sv_in = refs[:6]
+    tf, tv, route, kc_in, sf_in, sv_in = refs[:6]
     tables_in, outs = refs[6 : 6 + n], refs[6 + n : 10 + n]
-    raw, route, kc, sci = refs[10 + n : 14 + n]
-    tables = refs[14 + n : 14 + 2 * n]
-    gath, ysend, recv_flux, recv_var, rqs, rqr, lhs, alpha, maps, square, toep, hbuf, uh, ul = refs[14 + 2 * n : 28 + 2 * n]
-    ld_sem, tab_sem, xs, xr, ys, yr, rs, rr = refs[28 + 2 * n :]
+    raw, kc, sci = refs[10 + n : 13 + n]
+    tables = refs[13 + n : 13 + 2 * n]
+    gath, ysend, recv_flux, recv_var, rqs, rqr, lhs, alpha, maps, square, toep, hbuf, uh, ul = refs[13 + 2 * n : 27 + 2 * n]
+    ld_sem, tab_sem, xs, xr, ys, yr, rs, rr = refs[27 + 2 * n :]
     recv = (recv_flux, recv_var)
     ca, rh, tab = tables
     pick, pick2, term = (tab.at[lo:hi, 0:COLS] for lo, hi in ((0, 96), (96, 104), (104, 112)))
@@ -291,12 +291,11 @@
     for other in others:
         pl.semaphore_signal(barrier, inc=1, device_id=other, device_id_type=MESH)
     loads = fetch(
-        (tf.at[:, 0, :], tv.at[:, 0, :], route_in, kc_in, sf_in, sv_in),
-        (raw.at[0], raw.at[1], route, kc, sci.at[0], sci.at[1]),
+        (tf.at[:, 0, :], tv.at[:, 0, :], kc_in, sf_in, sv_in),
+        (raw.at[0], raw.at[1], kc, sci.at[0], sci.at[1]),
         ld_sem,
     )
     table_loads = fetch(tables_in, tables, tab_sem)
-    loads[2].wait()
     for k in range(5):
         want = jnp.int32(0)
         for t in range(2):
@@ -348,7 +347,7 @@
             group[-1].start()
         answers.append(group)
 
-    for one in loads[3:] + table_loads:
+    for one in loads[2:] + table_loads:
         one.wait()
     half = len(CUTS)
     last = p >= npatch - 2
@@ -411,11 +410,10 @@
     out = pl.pallas_call(
         difference_kernel,
         out_shape=(jax.ShapeDtypeStruct((TILE, TILE), F32),) * 4,
-        in_specs=[hbm] * (6 + N_TABLES),
+        in_specs=[hbm, hbm, pl.BlockSpec(memory_space=pltpu.SMEM)] + [hbm] * (3 + N_TABLES),
         out_specs=(pl.BlockSpec(memory_space=pltpu.VMEM),) * 4,
         scratch_shapes=[
             pltpu.VMEM((2, PAD, PAD), F32),
-            pltpu.SMEM((2, 5), jnp.int32),
             pltpu.VMEM((kernel_coefs.shape[1], 1, COLS), F32),
             pltpu.VMEM((2, 2, TILE, TILE), F32),
         ]
@@ -435,7 +433,7 @@
             pltpu.VMEM((2 * ROWS, 1024), F32),
             pltpu.VMEM((2 * DEGREES * ROWS, 256), BF16),
             pltpu.VMEM((2 * DEGREES * ROWS, 256), BF16),
-            dma((6,)),
+            dma((5,)),
             dma((N_TABLES,)),
             dma((n, 4)),
             dma((n, 4)),

time: 31.1 us -> 31.7 us (1.019)
  Pallas kernels: 29.1 us -> 29.7 us
    pallas_call x1, Pallas kernels: 29.1 us -> 29.7 us  [per_device(): pl.pallas_call(difference_kernel, out_shape=(jax.ShapeDtypeStruct((TILE,...]
where the time goes in v7:
time: 31.7 us; the launch traced here: 31.1 us
  Pallas kernels  29.7 us (94%)
  other arithmetic  0.72 us (2%)
  local copies, waits for them, and re-layouts  0.68 us (2%)
    pallas_call x1, Pallas kernels, per_device(): pl.pallas_call(difference_kernel, out_shape=(jax.ShapeDtypeStruct((TILE,...  29.7 us
    another operation x1, other arithmetic, per_device(): return jnp.stack(out).reshape(1, 2, 2, TILE, TILE)  0.72 us
    unnamed x2, local copies, waits for them, and re-layouts  0.68 us

profile of v7, /device:TPU:1, one launch (start us, length us, event | category | flops | bytes accessed | tf_op | source)
XLA Modules:
  0.0 31.1 jit_solution(5601300778305640204)
XLA Ops:
  0.0 0.0 copy-start
  0.0 0.7 %copy-done = s32[1,2,5]{2,1,0:T(2,128)S(1)} copy-done((s32[1,2,5]{2,1,0:T(2,128)S(1)}, s32[1,2,5]{2,1,0:T(2,128)}, u32[]{:S(2)}) %copy-start) | copy-done | bytes 64
  0.7 29.7 %difference.1 = (f32[128,128]{1,0:T(8,128)S(1)}, f32[128,128]{1,0:T(8,128)S(1)}, f32[128,128]{1,0:T(8,128)S(1)}, f32[128,128]{1,0:T(8,128)S(1)}) custom-call(f32[150,1,150]{2,1,0:T(1,128)} %bitcast.17, f32[150,1,150]{2,1,0:T(1,128)} %bitcast.18, s32[2,5]{1,0:T(2,128)S(1)} %bitcast.15, f32[189,1,192]{2,1,0:T(1,128)} %bitcast.16, f32[2,128,128]{2,1,0:T(8,128)} %bitcast.19, ...), custom_call_target="tpu_custom_call" | custom-call | tf_op jit(solution)/shard_map/difference/pallas_call | solution.py:410
  30.4 0.7 %pad_maximum_fusion = f32[4,128,128]{2,1,0:T(8,128)} fusion(f32[1,128,128]{2,1,0:T(8,128)S(1)} %bitcast.14, f32[1,128,128]{2,1,0:T(8,128)S(1)} %bitcast.13, f32[1,128,128]{2,1,0:T(8,128)S(1)} %bitcast.12, f32[1,128,128]{2,1,0:T(8,128)S(1)} %bitcast.11), kind=kLoop, calls=%fused_computation | loop fusion | flops 196608 | bytes 524288 | tf_op jit(solution)/shard_map/stack | solution.py:458
Async XLA Ops:
  0.0 0.7 %copy-start = (s32[1,2,5]{2,1,0:T(2,128)S(1)}, s32[1,2,5]{2,1,0:T(2,128)}, u32[]{:S(2)}) copy-start(s32[1,2,5]{2,1,0:T(2,128)} %param.14) | copy-start | bytes 124
